TPU v7x, 128 devices: a whole 4x4x4 slice. The times are simulated.
128 devices in a mesh: dp: 16 (over z_lo, y, core), tensor: 8 (over z_hi, x).
Axes of the slice: x: 4, y: 4, z: 4 (z_hi: 2, z_lo: 2; z = z_hi * 2 + z_lo), core: 2. Of those that a mesh axis runs over, the one named last changes fastest.
Arguments:
- tokens: bfloat16 [16384, 2048], P('dp'), may hold values from -6 to 6
- ln_gain: bfloat16 [2048], P('dp'), may hold values from 0.099609375 to 1.8984375
- ln_bias: bfloat16 [2048], P('dp'), may hold values from -2 to 2
- w_qkv: bfloat16 [2048, 3, 2048], P('dp', None, 'tensor'), may hold values from -0.125 to 0.125
- b_qkv: bfloat16 [3, 32, 64], P(None, 'tensor', 'dp'), may hold values from -2 to 2
- w_out: bfloat16 [2048, 2048], P('tensor', 'dp'), may hold values from -1 to 1
- b_out: bfloat16 [2048], P('dp'), may hold values from -2 to 2
- w_up: bfloat16 [2048, 8192], P('dp', 'tensor'), may hold values from -0.125 to 0.125
- b_up: bfloat16 [8, 1024], P('tensor', 'dp'), may hold values from -2 to 2
- w_down: bfloat16 [8192, 2048], P('tensor', 'dp'), may hold values from -0.0625 to 0.0625
- b_down: bfloat16 [2048], P('dp'), may hold values from -2 to 2
- cotangent: bfloat16 [16384, 2048], P('dp'), may hold values from -6 to 6
Outputs:
- mixed: bfloat16 [16384, 2048], P('dp')
- input_grad: bfloat16 [16384, 2048], P('dp')
- grad_ln_gain: float32 [2048], P('dp')
- grad_ln_bias: float32 [2048], P('dp')
- grad_w_qkv: float32 [2048, 3, 2048], P('dp', None, 'tensor')
- grad_b_qkv: float32 [3, 32, 64], P(None, 'tensor', 'dp')
- grad_w_out: float32 [2048, 2048], P('tensor', 'dp')
- grad_b_out: float32 [2048], P('dp')
- grad_w_up: float32 [2048, 8192], P('dp', 'tensor')
- grad_b_up: float32 [8, 1024], P('tensor', 'dp')
- grad_w_down: float32 [8192, 2048], P('tensor', 'dp')
- grad_b_down: float32 [2048], P('dp')
All inputs are finite; a program needn't handle non-finite values.
Results may differ from a plain program's by a relative error of at most 0.012.
Values may be sent and summed in bfloat16 or wider, within the bound.
A program may use at most 192 MiB of HBM per device.

v0:
```python
from functools import partial

import jax
import jax.numpy as jnp
from jax import lax
from jax.sharding import PartitionSpec as P

HD = 64
ROT = 32
LEN = 1024


norm_epsilon = 1e-05
rope_base = 10000.0


def rotary_tables(length, rot_dims):
    positions = jnp.arange(length, dtype=jnp.float32)
    frequency = rope_base ** (-jnp.arange(0, rot_dims, 2, dtype=jnp.float32) / rot_dims)
    angles = positions[:, None] * frequency[None, :]
    angles = jnp.concatenate([angles, angles], axis=-1)
    return (jnp.cos(angles)[:, None, :], jnp.sin(angles)[:, None, :])


def rotate(values_in, cosine_table, sine_table):
    rot_dims = cosine_table.shape[-1]
    half_dims = rot_dims // 2
    rotated_part = values_in[..., :rot_dims]
    turned = jnp.concatenate(
        [-rotated_part[..., half_dims:], rotated_part[..., :half_dims]], axis=-1
    )
    return jnp.concatenate(
        [rotated_part * cosine_table + turned * sine_table, values_in[..., rot_dims:]], axis=-1
    )


def rotate_back(grads_in, cosine_table, sine_table):
    rot_dims = cosine_table.shape[-1]
    half_dims = rot_dims // 2
    rotated_part = grads_in[..., :rot_dims]
    times_sine = rotated_part * sine_table
    turned = jnp.concatenate([times_sine[..., half_dims:], -times_sine[..., :half_dims]], axis=-1)
    return jnp.concatenate(
        [rotated_part * cosine_table + turned, grads_in[..., rot_dims:]], axis=-1
    )


def block_scores(queries, key_rows, row_start, block_rows, row_end, score_scale):
    query_block = queries[:, row_start:row_end]
    key_block = key_rows[:, :row_end]
    scores = (
        jnp.einsum("sqhe,skhe->shqk", query_block, key_block, preferred_element_type=jnp.float32)
        * score_scale
    )
    causal = (row_start + jnp.arange(block_rows))[:, None] >= jnp.arange(row_end)[None, :]
    return jnp.where(causal, scores, -1e30)


def attention_forward(queries, key_rows, value_rows, score_scale):
    length = queries.shape[1]
    block_rows = min(512, length)
    attended = []
    log_totals = []
    for block_index in range(length // block_rows):
        row_start = block_index * block_rows
        row_end = row_start + block_rows
        scores = block_scores(queries, key_rows, row_start, block_rows, row_end, score_scale)
        row_max = jnp.max(scores, axis=-1, keepdims=True)
        raised = jnp.exp(scores - row_max)
        row_total = jnp.sum(raised, axis=-1, keepdims=True)
        probs_low = (raised / row_total).astype(jnp.bfloat16)
        log_totals.append(row_max + jnp.log(row_total))
        attended.append(
            jnp.einsum(
                "shqk,skhe->sqhe",
                probs_low,
                value_rows[:, :row_end],
                preferred_element_type=jnp.float32,
            )
        )
    return (
        jnp.concatenate(attended, axis=1).astype(jnp.bfloat16),
        jnp.concatenate(log_totals, axis=2),
    )


def attention_backward(queries, key_rows, value_rows, grad_attended, log_totals, score_scale):
    length = queries.shape[1]
    block_rows = min(512, length)
    grad_queries = []
    grad_keys = jnp.zeros(key_rows.shape, jnp.float32)
    grad_values = jnp.zeros(value_rows.shape, jnp.float32)
    for block_index in range(length // block_rows):
        row_start = block_index * block_rows
        row_end = row_start + block_rows
        scores = block_scores(queries, key_rows, row_start, block_rows, row_end, score_scale)
        probs = jnp.exp(scores - log_totals[:, :, row_start:row_end])
        probs_low = probs.astype(jnp.bfloat16)
        grad_block = grad_attended[:, row_start:row_end]
        grad_probs = jnp.einsum(
            "sqhe,skhe->shqk",
            grad_block,
            value_rows[:, :row_end],
            preferred_element_type=jnp.float32,
        )
        inner = jnp.sum(probs * grad_probs, axis=-1, keepdims=True)
        grad_scores = (probs * (grad_probs - inner)).astype(jnp.bfloat16)
        grad_queries.append(
            jnp.einsum(
                "shqk,skhe->sqhe",
                grad_scores,
                key_rows[:, :row_end],
                preferred_element_type=jnp.float32,
            )
            * score_scale
        )
        key_terms = (
            jnp.einsum(
                "shqk,sqhe->skhe",
                grad_scores,
                queries[:, row_start:row_end],
                preferred_element_type=jnp.float32,
            )
            * score_scale
        )
        grad_keys = grad_keys.at[:, :row_end].add(key_terms)
        value_terms = jnp.einsum(
            "shqk,sqhe->skhe", probs_low, grad_block, preferred_element_type=jnp.float32
        )
        grad_values = grad_values.at[:, :row_end].add(value_terms)
    return (jnp.concatenate(grad_queries, axis=1), grad_keys, grad_values)


def norm_backward(grad_normed, normalized, inverse_std, gain_wide, upstream_wide):
    scaled = grad_normed * gain_wide
    grad_inputs = inverse_std * (
        scaled
        - jnp.mean(scaled, axis=-1, keepdims=True)
        - normalized * jnp.mean(scaled * normalized, axis=-1, keepdims=True)
    )
    return (upstream_wide + grad_inputs).astype(jnp.bfloat16)


def body(
    tokens, ln_gain, ln_bias, w_qkv, b_qkv, w_out, b_out, w_up, b_up, w_down, b_down, cotangent
):
    (
        gain_full,
        bias_full,
        qkv_full,
        qkv_bias_full,
        out_full,
        out_bias_full,
        up_full,
        up_bias_full,
        down_full,
        down_bias_full,
    ) = (
        lax.all_gather(ln_gain, "dp", axis=0, tiled=True),
        lax.all_gather(ln_bias, "dp", axis=0, tiled=True),
        lax.all_gather(w_qkv, "dp", axis=0, tiled=True),
        lax.all_gather(b_qkv, "dp", axis=2, tiled=True),
        lax.all_gather(w_out, "dp", axis=1, tiled=True),
        lax.all_gather(b_out, "dp", axis=0, tiled=True),
        lax.all_gather(w_up, "dp", axis=0, tiled=True),
        lax.all_gather(b_up, "dp", axis=1, tiled=True),
        lax.all_gather(w_down, "dp", axis=1, tiled=True),
        lax.all_gather(b_down, "dp", axis=0, tiled=True),
    )
    token_rows = tokens.shape[0]
    seq_count = token_rows // LEN
    heads_local = qkv_full.shape[2] // HD
    score_scale = HD ** (-0.5)
    inputs = tokens.astype(jnp.float32)
    row_mean = jnp.mean(inputs, axis=-1, keepdims=True)
    centred = inputs - row_mean
    row_variance = jnp.mean(centred * centred, axis=-1, keepdims=True)
    inverse_std = lax.rsqrt(row_variance + norm_epsilon)
    normalized = centred * inverse_std
    normed = (normalized * gain_full.astype(jnp.float32) + bias_full.astype(jnp.float32)).astype(
        jnp.bfloat16
    )
    projected = jnp.einsum(
        "td,dce->tce", normed, qkv_full, preferred_element_type=jnp.float32
    ) + qkv_bias_full.astype(jnp.float32).reshape(3, -1)
    projected = projected.reshape(seq_count, LEN, 3, heads_local, HD)
    cosine_table, sine_table = rotary_tables(LEN, ROT)
    queries = rotate(projected[:, :, 0], cosine_table, sine_table).astype(jnp.bfloat16)
    key_rows = rotate(projected[:, :, 1], cosine_table, sine_table).astype(jnp.bfloat16)
    value_rows = projected[:, :, 2].astype(jnp.bfloat16)
    attended, log_totals = attention_forward(queries, key_rows, value_rows, score_scale)
    attended_flat = attended.reshape(token_rows, -1)
    hidden_pre = jnp.dot(normed, up_full, preferred_element_type=jnp.float32) + up_bias_full.astype(
        jnp.float32
    ).reshape(-1)
    activated, gelu_pullback = jax.vjp(partial(jax.nn.gelu, approximate=True), hidden_pre)
    activated_low = activated.astype(jnp.bfloat16)
    branch_terms = jnp.dot(attended_flat, out_full, preferred_element_type=jnp.float32) + jnp.dot(
        activated_low, down_full, preferred_element_type=jnp.float32
    )
    bias_sum = out_bias_full.astype(jnp.float32) + down_bias_full.astype(jnp.float32)
    branch_total = lax.psum(branch_terms, "tensor")
    mixed = (inputs + branch_total + bias_sum).astype(jnp.bfloat16)
    gain_back, qkv_back, out_back, up_back, down_back = (
        lax.all_gather(ln_gain, "dp", axis=0, tiled=True),
        lax.all_gather(w_qkv, "dp", axis=0, tiled=True),
        lax.all_gather(w_out, "dp", axis=1, tiled=True),
        lax.all_gather(w_up, "dp", axis=0, tiled=True),
        lax.all_gather(w_down, "dp", axis=1, tiled=True),
    )
    upstream_wide = cotangent.astype(jnp.float32)
    grad_down = jnp.einsum(
        "tf,td->fd", activated_low, cotangent, preferred_element_type=jnp.float32
    )
    grad_out_w = jnp.einsum(
        "te,td->ed", attended_flat, cotangent, preferred_element_type=jnp.float32
    )
    grad_out_bias = jnp.sum(upstream_wide, axis=0)
    grad_act = jnp.einsum("td,fd->tf", cotangent, down_back, preferred_element_type=jnp.float32)
    grad_hidden = gelu_pullback(grad_act)[0].astype(jnp.bfloat16)
    grad_up = jnp.einsum("td,tf->df", normed, grad_hidden, preferred_element_type=jnp.float32)
    grad_up_bias = jnp.sum(grad_hidden.astype(jnp.float32), axis=0).reshape(1, -1)
    grad_attended = jnp.einsum(
        "td,ed->te", cotangent, out_back, preferred_element_type=jnp.float32
    ).astype(jnp.bfloat16)
    grad_attended = grad_attended.reshape(seq_count, LEN, heads_local, HD)
    grad_queries, grad_keys, grad_values = attention_backward(
        queries, key_rows, value_rows, grad_attended, log_totals, score_scale
    )
    grad_queries = rotate_back(grad_queries, cosine_table, sine_table).astype(jnp.bfloat16)
    grad_keys = rotate_back(grad_keys, cosine_table, sine_table).astype(jnp.bfloat16)
    grad_values = grad_values.astype(jnp.bfloat16)
    grad_proj = jnp.stack([grad_queries, grad_keys, grad_values], axis=2).reshape(token_rows, 3, -1)
    grad_qkv = jnp.einsum("td,tce->dce", normed, grad_proj, preferred_element_type=jnp.float32)
    grad_qkv_bias = jnp.sum(grad_proj.astype(jnp.float32), axis=0).reshape(3, heads_local, HD)
    grad_normed_part = jnp.einsum(
        "tce,dce->td", grad_proj, qkv_back, preferred_element_type=jnp.float32
    ) + jnp.einsum("tf,df->td", grad_hidden, up_back, preferred_element_type=jnp.float32)
    gain_wide = gain_back.astype(jnp.float32)
    grad_normed = lax.psum(grad_normed_part, "tensor")
    grad_gain = jnp.sum(grad_normed * normalized, axis=0)
    grad_norm_bias = jnp.sum(grad_normed, axis=0)
    input_grad = norm_backward(grad_normed, normalized, inverse_std, gain_wide, upstream_wide)
    (
        shard_gain,
        shard_norm_bias,
        shard_qkv,
        shard_qkv_bias,
        shard_out,
        shard_out_bias,
        shard_up,
        shard_up_bias,
        shard_down,
        shard_down_bias,
    ) = (
        lax.psum_scatter(grad_gain, "dp", scatter_dimension=0, tiled=True),
        lax.psum_scatter(grad_norm_bias, "dp", scatter_dimension=0, tiled=True),
        lax.psum_scatter(grad_qkv, "dp", scatter_dimension=0, tiled=True),
        lax.psum_scatter(grad_qkv_bias, "dp", scatter_dimension=2, tiled=True),
        lax.psum_scatter(grad_out_w, "dp", scatter_dimension=1, tiled=True),
        lax.psum_scatter(grad_out_bias, "dp", scatter_dimension=0, tiled=True),
        lax.psum_scatter(grad_up, "dp", scatter_dimension=0, tiled=True),
        lax.psum_scatter(grad_up_bias, "dp", scatter_dimension=1, tiled=True),
        lax.psum_scatter(grad_down, "dp", scatter_dimension=1, tiled=True),
        lax.psum_scatter(grad_out_bias, "dp", scatter_dimension=0, tiled=True),
    )
    return (
        mixed,
        input_grad,
        shard_gain,
        shard_norm_bias,
        shard_qkv,
        shard_qkv_bias,
        shard_out,
        shard_out_bias,
        shard_up,
        shard_up_bias,
        shard_down,
        shard_down_bias,
    )


def solution(mesh):
    in_specs = (
        P("dp", None),
        P("dp"),
        P("dp"),
        P("dp", None, "tensor"),
        P(None, "tensor", "dp"),
        P("tensor", "dp"),
        P("dp"),
        P("dp", "tensor"),
        P("tensor", "dp"),
        P("tensor", "dp"),
        P("dp"),
        P("dp", None),
    )
    out_specs = (
        P("dp", None),
        P("dp", None),
        P("dp"),
        P("dp"),
        P("dp", None, "tensor"),
        P(None, "tensor", "dp"),
        P("tensor", "dp"),
        P("dp"),
        P("dp", "tensor"),
        P("tensor", "dp"),
        P("tensor", "dp"),
        P("dp"),
    )
    return jax.shard_map(body, mesh=mesh, in_specs=in_specs, out_specs=out_specs, check_vma=False)
```

profile of v0, /device:TPU:0, one launch (start us, length us, event | category | flops | bytes accessed | tf_op | source)
XLA Modules:
  0.0 893.1 jit_solution(14411325499622404069)
XLA Ops:
  14.7 31.3 %all-reduce.2 = bf16[1024]{0:T(1024)(128)(2,1)S(1)} all-reduce(bf16[1024]{0:T(1024)(128)(2,1)S(1)} %dynamic-update-slice.10), channel_id=1, replica_groups=mesh['dp'=16,'tensor'=8] {'dp'}, use_global_device_ids=true, to_apply=%add.2 | all-reduce | flops 1024 | bytes 4096
  47.4 3.0 convert_reduce_fusion
  52.1 15.9 %all-gather = bf16[16,1,128]{2,1,0:T(2,128)(2,1)S(1)} all-gather(bf16[1,1,128]{2,1,0:T(2,128)(2,1)S(1)} %bitcast.179), channel_id=1, replica_groups=mesh['dp'=16,'tensor'=8] {'dp'}, dimensions={0}, use_global_device_ids=true | all-gather | bytes 4352 | tf_op jit(solution)/shard_map/all_gather | solution.py:159
  68.0 17.8 %all-gather.1 = bf16[16,1,128]{2,1,0:T(2,128)(2,1)S(1)} all-gather(bf16[1,1,128]{2,1,0:T(2,128)(2,1)S(1)} %bitcast.180), channel_id=1, replica_groups=mesh['dp'=16,'tensor'=8] {'dp'}, dimensions={0}, use_global_device_ids=true | all-gather | bytes 4352 | tf_op jit(solution)/shard_map/all_gather | solution.py:160
  85.8 16.4 %all_gather.38 = bf16[3,4,64]{1,0,2:T(4,128)(2,1)S(1)} all-gather(bf16[3,4,4]{1,0,2:T(4,128)(2,1)S(1)} %copy.58), channel_id=1, replica_groups=mesh['dp'=16,'tensor'=8] {'dp'}, dimensions={2}, use_global_device_ids=true | all-gather | bytes 1632 | tf_op jit(solution)/shard_map/all_gather | solution.py:162
  104.6 4.7 convolution_convert_fusion
  109.3 7.0 fusion.39
  127.9 3.5 multiply_reduce_fusion.2
  133.4 4.8 multiply_convert_fusion.1
  139.5 2.6 multiply_reduce_fusion
  148.6 3.0 fusion.59
  151.6 5.4 fusion.60
  157.1 10.0 %fusion.103 = f32[1024,1024]{1,0:T(8,128)} fusion(bf16[2048,1024]{1,0:T(8,128)(2,1)} %all-gather.13.cloned.1.call-done, bf16[1024,2048]{1,0:T(8,128)(2,1)} %param.24, f32[2048]{0:T(1024)S(1)} %bitcast.175, f32[2048]{0:T(1024)S(1)} %bitcast.167, f32[1024]{0:T(1024)S(1)} %copy-done.30, f32[1024]{0:T(1024)S(1)} %copy-done.28), kind=kOutput, calls=%fused_computation.160 | convolution fusion | flops 4307550208 | bytes 12607488 | tf_op jit(solution)/shard_map/dot_general | solution.py:193
  167.2 8.6 all-gather.15.cloned.1.call-done
  175.7 13.1 %convert_reduce_fusion.2 = (f32[1024]{0:T(1024)S(1)}, bf16[1024,1024]{1,0:T(8,128)(2,1)}) fusion(f32[1024,1024]{1,0:T(8,128)} %fusion.103, f32[1024]{0:T(1024)S(1)} %copy-done.41, bf16[1024,2048]{1,0:T(8,128)(2,1)} %param.35, bf16[1024,2048]{1,0:T(8,128)(2,1)} %all-gather.15.cloned.1.call-done), kind=kOutput, calls=%fused_computation.46 | convolution fusion | flops 4319083520 | bytes 14688256 | tf_op jit(solution)/shard_map/td,fd->tf/dot_general | solution.py:219
  190.0 8.6 fusion.99
  198.6 4.6 fusion.112
  203.2 5.7 bitcast_add_fusion
  208.9 4.5 convolution_add_fusion
  213.7 4.8 fusion.72
  218.6 9.0 %fusion.27 = f32[2048,3,256]{2,0,1:T(8,128)} fusion(bf16[1024,1,256]{2,0,1:T(8,128)(2,1)S(1)} %copy-done.13, bf16[1024,1,256]{2,0,1:T(8,128)(2,1)S(1)} %copy.65, bf16[1024,1,256]{2,0,1:T(8,128)(2,1)S(1)} %copy.64, bf16[1024,2048]{1,0:T(8,128)(2,1)} %param.24, f32[2048]{0:T(1024)S(1)} %bitcast.176, f32[2048]{0:T(1024)S(1)} %bitcast.168, ...), kind=kOutput, calls=%fused_computation.42 | convolution fusion | flops 3238526976 | bytes 12083200 | tf_op jit(solution)/shard_map/td,tce->dce/dot_general | solution.py:234
  227.7 11.9 %fusion.98 = f32[1024,2048]{1,0:T(8,128)} fusion(bf16[1024,2048]{1,0:T(8,128)(2,1)} %param.35, f32[1024,1024]{1,0:T(8,128)} %fusion.103, f32[1024]{0:T(1024)S(1)} %copy-done.41), kind=kOutput, calls=%fused_computation.157 | convolution fusion | flops 4305453056 | bytes 16781312 | tf_op jit(solution)/shard_map/tf,td->fd/dot_general | solution.py:212
  239.9 11.1 %fusion.101 = f32[2048,1024]{1,0:T(8,128)} fusion(bf16[1024,1024]{1,0:T(8,128)(2,1)} %get-tuple-element.87, bf16[1024,2048]{1,0:T(8,128)(2,1)} %param.24, f32[2048]{0:T(1024)S(1)} %bitcast.177, f32[2048]{0:T(1024)S(1)} %bitcast.169, f32[1024]{0:T(1024)S(1)} %copy-done.30, f32[1024]{0:T(1024)S(1)} %copy-done.28), kind=kOutput, calls=%fused_computation.159 | convolution fusion | flops 4307550208 | bytes 14704640 | tf_op jit(solution)/shard_map/td,tf->df/dot_general | solution.py:221
  252.3 18.3 %all-gather.2 = bf16[16,1,128]{2,1,0:T(2,128)(2,1)S(1)} all-gather(bf16[1,1,128]{2,1,0:T(2,128)(2,1)S(1)} %bitcast.181), channel_id=1, replica_groups=mesh['dp'=16,'tensor'=8] {'dp'}, dimensions={0}, use_global_device_ids=true | all-gather | bytes 4352 | tf_op jit(solution)/shard_map/all_gather | solution.py:164
  270.7 16.2 %all-gather.3 = bf16[16,1,128]{2,1,0:T(2,128)(2,1)S(1)} all-gather(bf16[1,1,128]{2,1,0:T(2,128)(2,1)S(1)} %bitcast.182), channel_id=1, replica_groups=mesh['dp'=16,'tensor'=8] {'dp'}, dimensions={0}, use_global_device_ids=true | all-gather | bytes 4352 | tf_op jit(solution)/shard_map/all_gather | solution.py:168
  288.6 307.5 %all-reduce.11.cloned.1.call-done = (f32[1024,2048]{1,0:T(8,128)}, f32[1024,2048]{1,0:T(8,128)}) async-done(((f32[1024,2048]{1,0:T(8,128)}, f32[1024,2048]{1,0:T(8,128)}), (f32[1024,2048]{1,0:T(8,128)}, f32[1024,2048]{1,0:T(8,128)})) %all-reduce.11.cloned.1.call-update) | async-done | bytes 16777232 | tf_op jit(solution)/shard_map/psum | solution.py:202
  596.1 7.9 fusion.11
  604.4 10.9 %convert_reduce_fusion.1 = (f32[2048]{0:T(1024)S(1)}, bf16[1024,2048]{1,0:T(8,128)(2,1)}, bf16[1024,2048]{1,0:T(8,128)(2,1)}) fusion(bf16[1024,2048]{1,0:T(8,128)(2,1)} %param.35, f32[1024]{0:T(1024)S(1)} %broadcast_multiply_fusion.1, f32[1024]{0:T(1024)S(1)} %copy-done.28, bf16[1024,2048]{1,0:T(8,128)(2,1)S(1)} %copy-done.4, ...), kind=kLoop, calls=%fused_computation.3 | loop fusion | flops 31455232 | bytes 33595392 | tf_op jit(solution)/shard_map/reduce_sum | solution.py:218
  615.3 55.1 %all-reduce.7 = (f32[2048]{0:T(1024)S(1)}, f32[2048]{0:T(1024)S(1)}, f32[3,4,64]{2,1,0:T(4,128)S(1)}, f32[2048]{0:T(1024)S(1)}) all-reduce(f32[2048]{0:T(1024)S(1)} %get-tuple-element.76, f32[2048]{0:T(1024)S(1)} %get-tuple-element.79, f32[3,4,64]{2,1,0:T(4,128)S(1)} %reshape.625, ...), channel_id=2, replica_groups=mesh['dp'=16,'tensor'=8] {'dp'}, use_global_device_ids=true, to_apply=%region_13.14.clone | all-reduce | flops 6912 | bytes 55296
  672.3 60.2 %reduce-scatter.9.cloned.1.call-done = f32[128,3,256]{2,0,1:T(8,128)} async-done(((f32[2048,3,256]{2,0,1:T(8,128)}), f32[128,3,256]{2,0,1:T(8,128)}) %reduce-scatter.9.cloned.1.call-update) | async-done | bytes 393232 | tf_op jit(solution)/shard_map/reduce_scatter | solution.py:258
  732.5 76.5 %reduce-scatter.15.cloned.1.call-done = f32[1024,128]{1,0:T(8,128)} async-done(((f32[1024,2048]{1,0:T(8,128)}), f32[1024,128]{1,0:T(8,128)}) %reduce-scatter.15.cloned.1.call-update) | async-done | bytes 524304 | tf_op jit(solution)/shard_map/reduce_scatter | solution.py:264
  809.0 76.3 %reduce-scatter.13.cloned.1.call-done = f32[128,1024]{1,0:T(8,128)} async-done(((f32[2048,1024]{1,0:T(8,128)}), f32[128,1024]{1,0:T(8,128)}) %reduce-scatter.13.cloned.1.call-update) | async-done | bytes 524304 | tf_op jit(solution)/shard_map/reduce_scatter | solution.py:262
  (187 shorter events, 39.7 us)
Async XLA Ops:
  7.2 97.4 %all-gather.11.cloned.1.call-start = ((), (), s32[]{:S(2)}) async-start(), calls=%async_computation.6 | async-start | bytes 1114112 | tf_op jit(solution)/shard_map/all_gather | solution.py:163
  7.9 101.4 %all-gather.9.cloned.1.call-start = ((), (), s32[]{:S(2)}) async-start(), calls=%async_computation.5 | async-start | bytes 3342336 | tf_op jit(solution)/shard_map/all_gather | solution.py:161
  9.7 147.4 %all-gather.13.cloned.1.call-start = ((), (), s32[]{:S(2)}) async-start(), calls=%async_computation.7 | async-start | bytes 4456448 | tf_op jit(solution)/shard_map/all_gather | solution.py:165
  10.5 165.3 %all-gather.15.cloned.1.call-start = ((), (), s32[]{:S(2)}) async-start(), calls=%async_computation.8 | async-start | bytes 4456448 | tf_op jit(solution)/shard_map/all_gather | solution.py:167
  11.0 276.2 %reduce-scatter.17.cloned.1.call-start = ((), (), s32[]{:S(2)}) async-start(), calls=%async_computation.13 | async-start | bytes 557056
  47.4 20.6 %copy-start.43 = (bf16[128]{0:T(256)(128)(2,1)S(1)}, bf16[128]{0:T(256)(128)(2,1)}, u32[]{:S(2)}) copy-start(bf16[128]{0:T(256)(128)(2,1)} %param.26) | copy-start | bytes 772
  50.8 58.5 %copy-start.27 = (f32[1024]{0:T(1024)}, f32[1024]{0:T(1024)S(1)}, u32[]{:S(2)}) copy-start(f32[1024]{0:T(1024)S(1)} %broadcast_multiply_fusion.3) | copy-start | bytes 12292
  52.1 57.2 %copy-start.29 = (f32[1024]{0:T(1024)}, f32[1024]{0:T(1024)S(1)}, u32[]{:S(2)}) copy-start(f32[1024]{0:T(1024)S(1)} %add_rsqrt_fusion) | copy-start | bytes 12292
  68.0 41.3 %copy-start.25 = (f32[16,1,128]{2,1,0:T(1,128)}, f32[16,1,128]{2,1,0:T(1,128)S(1)}, u32[]{:S(2)}) copy-start(f32[16,1,128]{2,1,0:T(1,128)S(1)} %convert_element_type.169) | copy-start | bytes 24580
  85.8 23.5 %copy-start.39 = (f32[16,1,128]{2,1,0:T(1,128)}, f32[16,1,128]{2,1,0:T(1,128)S(1)}, u32[]{:S(2)}) copy-start(f32[16,1,128]{2,1,0:T(1,128)S(1)} %convert_element_type.170) | copy-start | bytes 24580
  116.3 22.4 %copy-start.6 = (f32[1024,3,256]{0,2,1:T(8,128)}, f32[1024,3,256]{0,2,1:T(8,128)S(1)}, u32[]{:S(2)}) copy-start(f32[1024,3,256]{0,2,1:T(8,128)S(1)} %fusion.39) | copy-start | bytes 9437188
  116.4 11.4 %copy-start.14 = (bf16[1,1024,4,64]{1,3,2,0:T(8,128)(2,1)}, bf16[1,1024,4,64]{1,3,2,0:T(8,128)(2,1)S(1)}, u32[]{:S(2)}) copy-start(bf16[1,1024,4,64]{1,3,2,0:T(8,128)(2,1)S(1)} %fusion.97) | copy-start | bytes 1572868
  118.8 9.1 %copy-start.2 = (f32[4,512,512]{1,2,0:T(8,128)}, f32[4,512,512]{1,2,0:T(8,128)S(1)}, u32[]{:S(2)}) copy-start(f32[4,512,512]{1,2,0:T(8,128)S(1)} %get-tuple-element.114) | copy-start | bytes 12582916
  133.4 6.0 copy-start.1
  133.4 6.1 copy-start.12
  151.6 5.5 copy-start.26
  151.6 5.5 copy-start.28
  151.6 5.5 copy-start.30
  151.6 5.5 copy-start.40
  157.1 18.7 %copy-start.41 = (f32[1024]{0:T(1024)S(1)}, f32[1024]{0:T(1024)}, u32[]{:S(2)}) copy-start(f32[1024]{0:T(1024)} %add.200) | copy-start | bytes 12292
  189.9 406.2 %all-reduce.11.cloned.1.call-start = ((), (), s32[]{:S(2)}) async-start(), calls=%async_computation.14 | async-start | bytes 33554432 | tf_op jit(solution)/shard_map/psum | solution.py:202
  189.9 8.6 copy-start.46
  189.9 8.6 copy-start.49
  203.2 5.8 copy-start.18
  213.5 458.8 %reduce-scatter.11.cloned.1.call-start = ((), (), s32[]{:S(2)}) async-start(), calls=%async_computation.10 | async-start | bytes 2228224 | tf_op jit(solution)/shard_map/reduce_scatter | solution.py:260
  218.6 513.9 %reduce-scatter.9.cloned.1.call-start = ((), (), s32[]{:S(2)}) async-start(), calls=%async_computation.9 | async-start | bytes 6684672 | tf_op jit(solution)/shard_map/reduce_scatter | solution.py:258
  227.6 581.4 %reduce-scatter.15.cloned.1.call-start = ((), (), s32[]{:S(2)}) async-start(), calls=%async_computation.12 | async-start | bytes 8912896 | tf_op jit(solution)/shard_map/reduce_scatter | solution.py:264
  239.6 645.7 %reduce-scatter.13.cloned.1.call-start = ((), (), s32[]{:S(2)}) async-start(), calls=%async_computation.11 | async-start | bytes 8912896 | tf_op jit(solution)/shard_map/reduce_scatter | solution.py:262
  251.0 19.7 %copy-start.45 = (bf16[128]{0:T(256)(128)(2,1)S(1)}, bf16[128]{0:T(256)(128)(2,1)}, u32[]{:S(2)}) copy-start(bf16[128]{0:T(256)(128)(2,1)} %param.34) | copy-start | bytes 772
  596.1 7.9 copy-start.4
  596.1 8.3 copy-start.5
  671.0 214.8 %copy-start.48 = (f32[128]{0:T(128)}, f32[128]{0:T(128)S(1)}, u32[]{:S(2)}) copy-start(f32[128]{0:T(128)S(1)} %dynamic-slice.34) | copy-start | bytes 1540
  (28 other events, 69.2 us)
Sparse Core Ops, SparseCore 0:
  9.6 36.5 all-gather.10
  48.4 41.1 all-gather.8
  91.3 37.7 all-gather.12
  130.6 45.1 all-gather.14
  190.0 60.6 reduce-scatter.16
  253.5 342.4 all-reduce.10
  599.2 60.7 reduce-scatter.10
  663.1 69.3 reduce-scatter.8
  735.6 73.3 reduce-scatter.14
  812.0 73.2 reduce-scatter.12
where the time goes:
time: 898 us; the launch traced here: 893 us
  waiting for transfers between devices  531 us (59%)
  blocking collectives  171 us (19%)
  matrix products  119 us (13%)
  other arithmetic  36.9 us (4%)
  between operations  17.4 us (2%)
  local copies, waits for them, and re-layouts  17 us (2%)
    psum x1, waiting for transfers between devices, body(): branch_total = lax.psum(branch_terms, 'tensor')  307 us
    unnamed x2, blocking collectives  86.4 us
    reduce_scatter x1, waiting for transfers between devices, body(): lax.psum_scatter(grad_down, 'dp', scatter_dimension=1, tiled=True)  76.5 us
    reduce_scatter x1, waiting for transfers between devices, body(): lax.psum_scatter(grad_up, 'dp', scatter_dimension=0, tiled=True)  76.3 us
    reduce_scatter x1, waiting for transfers between devices, body(): lax.psum_scatter(grad_qkv, 'dp', scatter_dimension=0, tiled=True)  60.2 us
    all_gather x1, blocking collectives, body(): lax.all_gather(b_out, 'dp', axis=0, tiled=True)  18.3 us
  transfers between devices with their start and end apart: 10, of which 5 were waited for; matrix products, arithmetic and copies ran while one was open for 17% of the time, Pallas kernels for 0%

commit v1 on v0

v1 whole, which is shorter than its diff:
```python
from functools import partial

import jax
import jax.numpy as jnp
import numpy as np
from jax import lax
from jax.sharding import PartitionSpec as P
from jax.experimental import pallas as pl
from jax.experimental.pallas import tpu as pltpu

HD = 64
ROT = 32
LEN = 1024
norm_epsilon = 1e-05
rope_base = 10000.0
MESH = pl.DeviceIdType.MESH

def place():
    dp = lax.axis_index("dp"); tn = lax.axis_index("tensor")
    return dp % 2, (dp // 2) % 4, dp // 8, tn % 4, tn // 4

def peer(c, y, zl, x, zh):
    return (zl * 8 + y * 2 + c, zh * 4 + x)

RELS = [(0, 0), (0, 1), (0, 3), (0, 2), (1, 0), (1, 1), (1, 3), (1, 2)]

def enter(devices):
    bar = pltpu.get_barrier_semaphore()
    for d in devices:
        pl.semaphore_signal(bar, inc=1, device_id=d, device_id_type=MESH)
    pl.semaphore_wait(bar, len(devices))

class Gather:
    def __init__(s, shard, full, axis, ss, rs):
        s.axis, s.ss, s.rs, s.full = axis, ss, rs, full
        s.c, s.y, s.zl, x, zh = place()
        c, y, zl = s.c, s.y, s.zl
        s.total = shard.shape[1 if axis == 2 else 0]
        s.shard = shard
        s.up = peer(c, (y + 1) % 4, zl, x, zh); s.down = peer(c, (y + 3) % 4, zl, x, zh)
        s.z = peer(c, y, 1 - zl, x, zh); s.sib = peer(1 - c, y, zl, x, zh)
        s.sends = []
    def slot(s, dz, dy, c=None, half=None):
        c = s.c if c is None else c
        d = ((s.zl + dz) % 2) * 8 + ((s.y + dy) % 4) * 2 + c
        n = s.total if half is None else s.total // 2
        lo = 0 if half is None else half * n
        if s.axis == 0: return s.full.at[pl.ds(pl.multiple_of(d * s.total + lo, 16), n)]
        if s.axis == 2: return s.full.at[:, pl.ds(pl.multiple_of(d * s.total + lo, 16), n)]
        return s.full.at[pl.ds(lo, n), pl.ds(pl.multiple_of(d * 128, 128), 128)]
    def send(s, kind, src, dst, dev):
        cp = pltpu.make_async_remote_copy(src, dst, s.ss.at[kind], s.rs.at[kind], device_id=dev, device_id_type=MESH)
        cp.start(); s.sends.append(cp)
    def got(s, kind, dst):
        pltpu.make_async_remote_copy(dst, dst, s.ss.at[kind], s.rs.at[kind], device_id=s.sib, device_id_type=MESH).wait_recv()
    def start(s):
        own = s.slot(0, 0)
        s.send(0, s.shard, own, s.up); s.send(1, s.shard, own, s.down); s.send(2, s.shard, own, s.z)
        s.send(8, s.shard, own, s.sib)
    def relay(s, rel):
        b = s.slot(*RELS[rel]); s.send(8 + rel, b, b, s.sib)
    def serve(s):
        a = s.slot(0, 3); s.got(0, a); h = s.slot(0, 3, half=0); s.send(5, h, h, s.up)
        b = s.slot(0, 1); s.got(1, b); h = s.slot(0, 1, half=1); s.send(6, h, h, s.down)
        z = s.slot(1, 0); s.got(2, z); s.send(3, z, z, s.up); s.send(4, z, z, s.down)
        s.relay(2); s.relay(1); s.relay(4)
    def serve2(s):
        s.got(5, s.slot(0, 2, half=0)); s.got(6, s.slot(0, 2, half=1))
        f = s.slot(0, 2); s.send(7, f, f, s.z); s.relay(3)
    def serve3(s):
        s.got(3, s.slot(1, 3)); s.relay(6)
        s.got(4, s.slot(1, 1)); s.relay(5)
        s.got(7, s.slot(1, 2)); s.relay(7)
    def arrived(s):
        for r in range(8): s.got(8 + r, s.slot(*RELS[r], c=1 - s.c))

f32 = jnp.float32
bf16 = jnp.bfloat16

def by_rows(rows, step, fn):
    def go(i, carry):
        fn(pl.ds(pl.multiple_of(i * step, step), step))
        return carry
    lax.fori_loop(0, rows // step, go, 0)

def add_into(dst, terms, rows, step, lo=0):
    def go(r):
        if lo: r = pl.ds(pl.multiple_of(r.start + lo, step), step)
        total = terms[0][r, :].astype(f32)
        for t in terms[1:]: total = total + t[r, :].astype(f32)
        dst[r, :] = total.astype(dst.dtype)
    by_rows(rows, step, go)

class Link:
    def __init__(s, ss, rs):
        s.ss, s.rs, s.sends = ss, rs, []
        c, y, zl, x, zh = s.at = place()
        s.c, s.y, s.zl, s.x, s.zh = s.at
        s.sib = peer(1 - c, y, zl, x, zh)
        s.yu, s.yd, s.yf = (peer(c, (y + k) % 4, zl, x, zh) for k in (1, 3, 2))
        s.zn = peer(c, y, 1 - zl, x, zh)
        s.xu, s.xd, s.xf = (peer(c, y, zl, (x + k) % 4, zh) for k in (1, 3, 2))
        s.zf = peer(c, y, zl, x, 1 - zh)
    def send(s, kind, src, dst, dev):
        cp = pltpu.make_async_remote_copy(src, dst, s.ss.at[kind], s.rs.at[kind], device_id=dev, device_id_type=MESH)
        cp.start(); s.sends.append(cp)
    def got(s, kind, dst):
        pltpu.make_async_remote_copy(dst, dst, s.ss.at[kind], s.rs.at[kind], device_id=s.sib, device_id_type=MESH).wait_recv()
    def drain(s):
        for cp in s.sends: cp.wait_send()

class TensorSum(Link):
    def __init__(s, b, f, t1, t2, zs, zr, ss, rs):
        super().__init__(ss, rs)
        s.b, s.f, s.t1, s.t2, s.zs, s.zr = b, f, t1, t2, zs, zr
    def blk(s, zh, dx): return s.b.at[zh * 4 + (s.x + dx) % 4]
    LO, HI = pl.ds(0, 64), pl.ds(64, 64)
    def start_far(s): s.send(0, s.blk(1 - s.zh, 2), s.f, s.zf)
    def start_near(s):
        o = 1 - s.zh
        s.send(1, s.blk(o, 1), s.t2.at[0, o], s.xu); s.send(2, s.blk(o, 3), s.t2.at[1, o], s.xd)
        s.send(3, s.blk(s.zh, 1).at[s.HI], s.t2.at[0, s.zh, s.HI], s.xu); s.send(4, s.blk(s.zh, 3).at[s.LO], s.t2.at[1, s.zh, s.LO], s.xd)
    def middle(s):
        s.got(0, s.f); add_into(s.f, [s.f, s.blk(s.zh, 2)], 128, 32)
        s.send(5, s.f.at[s.LO], s.t1.at[s.LO], s.xu); s.send(6, s.f.at[s.HI], s.t1.at[s.HI], s.xd)
    def middle2(s):
        s.got(5, s.t1.at[s.LO]); add_into(s.t1, [s.t1, s.blk(s.zh, 1)], 64, 32)
        s.send(7, s.t1.at[s.LO], s.t2.at[0, s.zh, s.LO], s.xu)
        s.got(6, s.t1.at[s.HI]); add_into(s.t1, [s.t1, s.blk(s.zh, 3)], 64, 32, lo=64)
        s.send(8, s.t1.at[s.HI], s.t2.at[1, s.zh, s.HI], s.xd)
    def last(s):
        o = 1 - s.zh
        s.got(1, s.t2.at[0, o]); s.got(2, s.t2.at[1, o])
        add_into(s.zs, [s.blk(o, 0), s.t2.at[0, o], s.t2.at[1, o]], 128, 32)
        s.send(9, s.zs, s.zr, s.zf)
    def total(s, r):
        return (s.blk(s.zh, 0)[r, :].astype(f32) + s.t2.at[0, s.zh][r, :].astype(f32)
                + s.t2.at[1, s.zh][r, :].astype(f32) + s.zr[r, :].astype(f32))
    def arrived(s):
        z = s.zh
        s.got(3, s.t2.at[0, z, s.HI]); s.got(4, s.t2.at[1, z, s.LO]); s.got(7, s.t2.at[0, z, s.LO]); s.got(8, s.t2.at[1, z, s.HI])
        s.got(9, s.zr)

class TensorGather(Link):
    def __init__(s, o, ss, rs):
        super().__init__(ss, rs); s.o = o
    def blk(s, zh, dx): return s.o.at[zh * 4 + (s.x + dx) % 4]
    LO, HI = pl.ds(0, 64), pl.ds(64, 64)
    def start(s, own):
        b = s.blk(s.zh, 0)
        s.send(0, own, b, s.xu); s.send(1, own, b, s.xd); s.send(2, own, b, s.zf)
    def middle(s):
        b = s.blk(s.zh, 3); s.got(0, b); s.send(3, b.at[s.LO], b.at[s.LO], s.xu)
        b = s.blk(s.zh, 1); s.got(1, b); s.send(4, b.at[s.HI], b.at[s.HI], s.xd)
        b = s.blk(1 - s.zh, 0); s.got(2, b); s.send(5, b, b, s.xu); s.send(6, b, b, s.xd)
    def far(s):
        b = s.blk(s.zh, 2); s.got(3, b.at[s.LO]); s.got(4, b.at[s.HI]); s.send(7, b, b, s.zf)
    def finish(s):
        o = 1 - s.zh
        s.got(5, s.blk(o, 3)); s.got(6, s.blk(o, 1)); s.got(7, s.blk(o, 2))

class SmallSum(Link):
    def __init__(s, v, rc, rz, ry, rx, rt, acc, out, ss, rs):
        super().__init__(ss, rs)
        s.v, s.rc, s.rz, s.ry, s.rx, s.rt, s.acc, s.out = v, rc, rz, ry, rx, rt, acc, out
    def a(s): s.send(0, s.v.at[1 - s.c], s.rc, s.sib)
    def b(s):
        s.got(0, s.rc); s.rc[...] = s.rc[...] + s.v[s.c]
        s.send(1, s.rc.at[1 - s.zl], s.rz, s.zn)
    def c_(s):
        s.got(1, s.rz); s.rz[...] = s.rz[...] + s.rc[s.zl]
        s.send(2, s.rz.at[(s.y + 1) % 4], s.ry.at[0], s.yu); s.send(3, s.rz.at[(s.y + 3) % 4], s.ry.at[1], s.yd)
        s.send(4, s.rz.at[(s.y + 2) % 4], s.ry.at[2], s.yf)
    def d(s):
        for k in range(3): s.got(2 + k, s.ry.at[k])
        s.acc[0] = s.rz[s.y] + s.ry[0] + s.ry[1] + s.ry[2]
        s.send(5, s.acc.at[0], s.rx.at[0], s.xu); s.send(6, s.acc.at[0], s.rx.at[1], s.xd); s.send(7, s.acc.at[0], s.rx.at[2], s.xf)
    def e(s):
        for k in range(3): s.got(5 + k, s.rx.at[k])
        s.acc[1] = s.acc[0] + s.rx[0] + s.rx[1] + s.rx[2]
        s.send(8, s.acc.at[1], s.rt, s.zf)
    def f(s):
        s.got(8, s.rt)
        first = lax.broadcasted_iota(jnp.int32, (16, 128), 0) < 2
        s.out[...] = jnp.where(first, s.acc[1] + s.rt[...], s.acc[0])

def peers_all():
    c, y, zl, x, zh = place()
    return ([peer(1 - c, y, zl, x, zh), peer(c, y, 1 - zl, x, zh), peer(c, y, zl, x, 1 - zh)]
            + [peer(c, (y + k) % 4, zl, x, zh) for k in (1, 2, 3)] + [peer(c, y, zl, (x + k) % 4, zh) for k in (1, 2, 3)])

def norm_back_rows(r, gn, tokens, cot, gain, out, sums):
    x = tokens[r, :].astype(f32)
    mean = jnp.mean(x, axis=-1, keepdims=True); cen = x - mean
    inv = lax.rsqrt(jnp.mean(cen * cen, axis=-1, keepdims=True) + 1e-5)
    xh = cen * inv
    n = x.shape[0] // 8
    sums[0] += jnp.sum((gn * xh).reshape(n, 8, 2048), axis=0)
    sums[1] += jnp.sum(gn.reshape(n, 8, 2048), axis=0)
    sc = gn * gain
    ig = cot[r, :].astype(f32) + inv * (sc - jnp.mean(sc, axis=-1, keepdims=True) - xh * jnp.mean(sc * xh, axis=-1, keepdims=True))
    out[r, :] = ig.astype(bf16)

PLAN = ("v0", "q0", "v1", "o0", "q1", "v2", "o1", "v3", "q2", "first", "u0", "o2", "vectors", "q3", "n0", "d0", "n1", "Aq", "n2", "u1",
        "Wq", "n3", "sn", "o3", "p0", "p1", "p2", "p3", "Ao", "d1", "Wo", "u2", "ga", "a3x", "a3y", "a2x", "u3", "d2", "a2y", "a1x",
        "a1y", "Au", "a0x", "a0y", "sa", "k", "sg", "Wu", "h0", "d3", "h1", "h2", "h3")

def NT(a, b): return lax.dot_general(a, b, (((1,), (1,)), ((), ())), preferred_element_type=f32)
def NN(a, b): return lax.dot_general(a, b, (((1,), (0,)), ((), ())), preferred_element_type=f32)
def TN(a, b): return lax.dot_general(a, b, (((0,), (0,)), ((), ())), preferred_element_type=f32)

def rotary_tables():
    pos = np.arange(LEN, dtype=np.float32)
    freq = (np.float32(rope_base) ** (-np.arange(0, ROT, 2, dtype=np.float32) / np.float32(ROT))).astype(np.float32)
    ang = (pos[:, None] * freq[None, :]).astype(np.float32)
    cos, sin = np.cos(ang).astype(np.float32), np.sin(ang).astype(np.float32)
    one, zero = np.ones((LEN, 32), np.float32), np.zeros((LEN, 16), np.float32)
    c = np.concatenate([cos, cos, one], 1)
    s1 = np.concatenate([-sin, zero, zero, zero], 1)
    s2 = np.concatenate([zero, sin, zero, zero], 1)
    return np.stack([np.concatenate([t, t], 1) for t in (c, s1, s2)])

def turn(u, tab, r, sign):
    other = pltpu.roll(u, 112, 1) * tab[1, r, :] + pltpu.roll(u, 16, 1) * tab[2, r, :]
    straight = u * tab[0, r, :]
    return straight + other if sign > 0 else straight - other


def pack(vec, gain, lbias, bout, bdown, bup, bqkv):
    dp = lax.axis_index("dp")
    k = lax.broadcasted_iota(jnp.int32, (64, 128), 0); l = lax.broadcasted_iota(jnp.int32, (64, 128), 1)
    up = NN(bup[...], ((l % 64 == k) & (l // 64 == dp % 2)).astype(bf16))
    k4 = k[0:4]; l4 = l[0:4]
    on = (l4 % 4 == k4) & ((l4 % 64) // 4 == dp)
    rows = [gain[...].astype(f32), lbias[...].astype(f32), bout[...].astype(f32), bdown[...].astype(f32), up]
    for j in range(3):
        lo = NN(bqkv[j], (on & (l4 < 64)).astype(bf16)); hi = NN(bqkv[j], (on & (l4 >= 64)).astype(bf16))
        rows += [lo[0:1] + hi[1:2], lo[2:3] + hi[3:4]]
    vec[...] = jnp.concatenate(rows + [jnp.zeros((21, 128), f32)], 0).astype(bf16)

def forward_kernel(gain_s, lbias_s, bout_s, bdown_s, bup_s, bqkv_s, wq, wout, wup, wdown, tok_h, cot_h, tab_h,
                   vecs, wq_f, wout_f, wup_f, wdown_f, rows_h, nrm_h, att_h, act_h, dact_h, gp_h,
                   vec, tab, vv, wqv, woutv, wupv, tok, cot, nrm, rowsv, bqkv, bup, q, k, v, ga, att, dk, dv, gp, act, dact,
                   ss, rs, ls, ld):
    c, y, zl, x, zh = place()
    loads = {}
    def load(i, src, dst):
        loads[i] = pltpu.make_async_copy(src, dst, ld.at[i]); loads[i].start()
    load(0, tok_h, tok); load(1, cot_h, cot); load(12, tab_h, tab)
    pack(vec, gain_s, lbias_s, bout_s, bdown_s, bup_s, bqkv_s)
    enter([peer(c, (y + 1) % 4, zl, x, zh), peer(c, (y + 3) % 4, zl, x, zh), peer(c, y, 1 - zl, x, zh), peer(1 - c, y, zl, x, zh)])
    gv, gq, go, gu, gd = every = [Gather(a, b, ax, ss.at[i], rs.at[i]) for i, (a, b, ax) in enumerate(
        [(vec, vecs, 0), (wq, wq_f, 2), (wout, wout_f, 1), (wup, wup_f, 0), (wdown, wdown_f, 1)])]
    local = [pltpu.make_async_copy(g.shard, g.slot(0, 0), ls.at[i]) for i, g in enumerate(every)]
    for cp in local: cp.start()

    def norm(lo, hi):
        gain, bias = rowsv[0:1, :], rowsv[1:2, :]
        def go_(i, carry):
            r = pl.ds(pl.multiple_of(lo + i * 32, 32), 32)
            a = tok[r, :].astype(f32)
            cen = a - jnp.mean(a, axis=-1, keepdims=True)
            inv = lax.rsqrt(jnp.mean(cen * cen, axis=-1, keepdims=True) + norm_epsilon)
            nrm[r, :] = (cen * inv * gain + bias).astype(bf16)
            return carry
        lax.fori_loop(0, (hi - lo) // 32, go_, 0)

    def project(lo, hi):
        def go_(i, carry):
            r = pl.ds(pl.multiple_of(lo + i * 256, 256), 256)
            n = nrm[r, :]
            for j, dst in enumerate((q, k, v)):
                p = NN(n, wqv[j])
                for h in range(2):
                    u = p[:, h * 128:(h + 1) * 128] + bqkv[2 * j + h:2 * j + h + 1, :]
                    dst[h, r, :] = (u if j == 2 else turn(u, tab, r, 1)).astype(bf16)
            return carry
        lax.fori_loop(0, (hi - lo) // 256, go_, 0)

    def grad_attended():
        def go_(i, carry):
            r = pl.ds(pl.multiple_of(i * 256, 256), 256)
            p = NT(cot[r, :], woutv[...])
            ga[0, r, :] = p[:, 0:128].astype(bf16); ga[1, r, :] = p[:, 128:256].astype(bf16)
            return carry
        lax.fori_loop(0, 4, go_, 0)

    def attention(i):
        lax.fori_loop(0, 2, lambda p, carry: attention_pair(i, p, carry), 0)
    def attention_pair(i, p, carry=0):
            n = (i + 1) * 256
            r = pl.ds(i * 256, 256)
            cols = pl.ds(pl.multiple_of(p * 128, 128), 128)
            a_, d_, tk, tv = 0.0, 0.0, 0.0, 0.0
            for hh in range(2):
                m = ((lax.broadcasted_iota(jnp.int32, (1, 128), 1) // 64) == hh).astype(bf16)
                kk = k[p, 0:n] * m; w = v[p, 0:n] * m; qq = q[p, r] * (m * 0.125); gg = ga[p, r] * m
                s = NT(kk, qq)
                key = lax.broadcasted_iota(jnp.int32, (256, 256), 0); row = lax.broadcasted_iota(jnp.int32, (256, 256), 1)
                diag = jnp.where(row >= key, s[n - 256:], -1e30)
                s = diag if i == 0 else jnp.concatenate([s[:n - 256], diag], 0)
                e = jnp.exp(s - jnp.max(s, 0, keepdims=True))
                pr = e * (1.0 / jnp.sum(e, 0, keepdims=True))
                low = pr.astype(bf16)
                dp = NT(w, gg)
                ds = (pr * (dp - jnp.sum(pr * dp, 0, keepdims=True))).astype(bf16)
                a_ = a_ + TN(low, w); d_ = d_ + TN(ds, kk)
                tk = tk + NN(ds, qq); tv = tv + NN(low, gg)
            att[r, cols] = a_.astype(bf16)
            gp[r, cols] = turn(d_ * 0.125, tab, r, -1).astype(bf16)
            if i == 3: dk[p] = tk; dv[p] = tv
            else:
                dk[p, 0:n] += tk; dv[p, 0:n] += tv
            return carry

    def keys_done():
        def go_(i, carry):
            r = pl.ds(pl.multiple_of(i * 256, 256), 256)
            for p in range(2):
                gp[r, 256 + p * 128:384 + p * 128] = turn(dk[p, r], tab, r, -1).astype(bf16)
                gp[r, 512 + p * 128:640 + p * 128] = dv[p, r].astype(bf16)
            return carry
        lax.fori_loop(0, 4, go_, 0)

    def hidden(lo, hi):
        def go_(i, carry):
            r = pl.ds(pl.multiple_of(lo + i * 256, 256), 256)
            n = nrm[r, :]
            for j in range(4):
                cols = pl.ds(j * 256, 256)
                h = NN(n, wupv[:, cols]) + bup[0:1, cols]
                h2 = h * h
                t = jnp.tanh(0.7978845608028654 * h * (1.0 + 0.044715 * h2))
                act[r, cols] = (0.5 * h * (1.0 + t)).astype(bf16)
                dact[r, cols] = (0.5 * (1.0 + t) + 0.5 * h * (1.0 - t * t) * (0.7978845608028654 * (1.0 + 0.134145 * h2))).astype(bf16)
            return carry
        lax.fori_loop(0, (hi - lo) // 256, go_, 0)

    def first():
        gv.arrived(); local[0].wait(); load(2, vecs, vv)
    def vectors():
        loads[2].wait(); loads[0].wait()
        bq, bu = jnp.zeros((6, 128), f32), None
        for d in range(16):
            t = vv[pl.ds(d * 32, 32), :].astype(f32)
            cols = pl.ds(d * 128, 128)
            rowsv[0:1, cols] = t[0:1]; rowsv[1:2, cols] = t[1:2]; rowsv[2:3, cols] = t[2:3] + t[3:4]
            bq = bq + t[5:11]
            if d % 2 == 0: bu = t[4:5]
            else: bup[0:1, pl.ds((d // 2) * 128, 128)] = bu + t[4:5]
        bqkv[0:6, :] = bq
        load(6, rowsv, rows_h)
    def have_q():
        gq.arrived(); local[1].wait(); load(3, wq_f, wqv)
    def have_o():
        go.arrived(); local[2].wait(); load(4, wout_f, woutv)
    def have_u():
        gu.arrived(); local[3].wait(); load(7, wup_f, wupv)
    steps = {"first": first, "vectors": vectors, "Aq": have_q, "Ao": have_o, "Au": have_u,
             "Wq": lambda: (loads[3].wait(), loads[12].wait()), "Wo": lambda: (loads[4].wait(), loads[1].wait()), "Wu": lambda: loads[7].wait(),
             "ga": grad_attended, "k": keys_done, "sn": lambda: load(5, nrm, nrm_h), "sa": lambda: load(8, att, att_h), "sg": lambda: load(9, gp, gp_h)}
    for i in range(4):
        steps["n%d" % i] = partial(norm, i * 256, i * 256 + 256)
        steps["p%d" % i] = partial(project, i * 256, i * 256 + 256)
        steps["h%d" % i] = partial(hidden, i * 256, i * 256 + 256)
        steps["a%d" % i] = partial(attention, i)
        for p in range(2): steps["a%d%s" % (i, "xy"[p])] = partial(attention_pair, i, p)
    for nm, g in (("v", gv), ("q", gq), ("o", go), ("u", gu), ("d", gd)):
        steps[nm + "0"], steps[nm + "1"], steps[nm + "2"], steps[nm + "3"] = g.start, g.serve, g.serve2, g.serve3
    for name in PLAN: steps[name]()
    load(10, act, act_h); load(11, dact, dact_h)
    gd.arrived()
    for i in (5, 6, 8, 9, 10, 11): loads[i].wait()
    local[4].wait()
    for g in (gv, gq, go, gu, gd):
        for cp in g.sends: cp.wait_send()

def forward(vectors, wq, wout, wup, wdown, tokens, cot, tab):
    A = pl.BlockSpec(memory_space=pl.ANY); V = pl.BlockSpec(memory_space=pltpu.VMEM)
    S = jax.ShapeDtypeStruct
    vm = lambda sh, t=bf16: pltpu.VMEM(sh, t)
    return pl.pallas_call(forward_kernel,
        out_shape=[S((512, 128), bf16), S((3, 2048, 256), bf16), S((256, 2048), bf16), S((2048, 1024), bf16), S((1024, 2048), bf16),
                   S((8, 2048), f32), S((1024, 2048), bf16), S((1024, 256), bf16), S((1024, 1024), bf16), S((1024, 1024), bf16), S((1024, 768), bf16)],
        in_specs=[V] * 6 + [A] * 7, out_specs=[A] * 11,
        scratch_shapes=[vm((32, 128)), vm((3, 1024, 128), f32), vm((512, 128)), vm((3, 2048, 256)), vm((256, 2048)), vm((2048, 1024)), vm((1024, 2048)), vm((1024, 2048)), vm((1024, 2048)),
                        vm((8, 2048), f32), vm((8, 128), f32), vm((8, 1024), f32), vm((2, 1024, 128)), vm((2, 1024, 128)), vm((2, 1024, 128)), vm((2, 1024, 128)),
                        vm((1024, 256)), vm((2, 1024, 128), f32), vm((2, 1024, 128), f32), vm((1024, 768)), vm((1024, 1024)), vm((1024, 1024)),
                        pltpu.SemaphoreType.DMA((5, 16)), pltpu.SemaphoreType.DMA((5, 16)), pltpu.SemaphoreType.DMA((5,)), pltpu.SemaphoreType.DMA((13,))],
        compiler_params=pltpu.CompilerParams(collective_id=1, has_side_effects=True, vmem_limit_bytes=60 << 20),
        name="gather_and_forward")(*vectors, wq, wout, wup, wdown, tokens, cot, tab)

class Scatter(Link):
    def __init__(s, g, sib, mid, ss, rs, width):
        super().__init__(ss, rs)
        s.g, s.b, s.m, s.w = g, sib, mid, width
    def to_sibling(s, k):
        return pltpu.make_async_remote_copy(s.g.at[k, 1 - s.c, :, pl.ds(0, s.w)], s.b.at[k], s.ss.at[k], s.rs.at[k],
                                            device_id=s.sib, device_id_type=MESH)
    def produce(s, lhs, rhs_list):
        def go(k, carry):
            chip = (k % 2) * 4 + (s.y + 2 + 3 * (k // 2)) % 4
            a = lhs[:, pl.ds(pl.multiple_of(chip * 256, 256), 256)]
            at = 0
            for rhs in rhs_list:
                n = rhs.shape[1]
                for lo in range(0, n, 512):
                    w = min(512, n - lo)
                    p = TN(a, rhs[:, lo:lo + w]).astype(bf16)
                    s.g[k, 0, :, at:at + w] = p[0:128]; s.g[k, 1, :, at:at + w] = p[128:256]
                    at += w
            s.to_sibling(k).start()
            return carry
        lax.fori_loop(0, 8, go, 0)
    def pairs(s):
        def go(k, carry):
            s.to_sibling(k).wait()
            mine = s.g.at[k, s.c]; dst = s.b.at[k]
            def rows(i, cc):
                r = pl.ds(pl.multiple_of(i * 32, 32), 32)
                dst[r, :] = (dst[r, :].astype(f32) + mine[r, 0:s.w].astype(f32)).astype(bf16)
                return cc
            lax.fori_loop(0, 4, rows, 0)
            return carry
        lax.fori_loop(0, 8, go, 0)
    def serve1(s):
        s.send(8, s.b.at[0], s.m.at[0], s.yu); s.send(9, s.b.at[1], s.m.at[1], s.yd)
        s.send(10, s.b.at[3], s.m.at[4], s.yu); s.send(11, s.b.at[6], s.m.at[2], s.yd)
    def serve2(s):
        s.got(8, s.m.at[0]); add_into(s.b.at[2], [s.b.at[2], s.m.at[0]], 128, 32); s.send(12, s.b.at[2], s.m.at[3], s.yu)
        s.got(9, s.m.at[1]); add_into(s.b.at[7], [s.b.at[7], s.m.at[1]], 128, 32); s.send(13, s.b.at[7], s.m.at[5], s.yd)
    def serve3(s):
        for k, j in ((10, 4), (11, 2), (12, 3), (13, 5)): s.got(k, s.m.at[j])
        o = 1 - s.zl; b = s.b.at[4 + o]
        add_into(b, [b, s.m.at[2 + 2 * o], s.m.at[3 + 2 * o]], 128, 32); s.send(14, b, s.m.at[6], s.zn)
    def serve4(s, put):
        s.got(14, s.m.at[6])
        z = s.zl
        terms = (s.b.at[4 + z], s.m.at[2 + 2 * z], s.m.at[3 + 2 * z], s.m.at[6])
        def go(r):
            t = terms[0][r, :].astype(f32)
            for q in terms[1:]: t = t + q[r, :].astype(f32)
            put(r, t)
        by_rows(128, 32, go)

def backward_kernel(wq_f, wout_f, wup_f, wdown_f, rows_h, nrm_h, att_h, act_h, dact_h, gp_h, cot_h, tok_h,
                    mixed, ingrad, o2, oup, oq, osv,
                    woutv, wdownv, wqc, wuc, cot, nrm, att, act, gh, gp, rowsv, tok, brp, gnp, own,
                    fa, t1a, t2a, zsa, zra, fb, t1b, t2b, zsb, zrb, g, sib2, m2, sibu, mu, sibq, mq,
                    v, rc, rz, ry, rx, rt, acc, sums, ss, rs, ld):
    c, y, zl, x, zh = place()
    t_own = zh * 4 + x
    loads = {}
    def load(i, src, dst):
        loads[i] = pltpu.make_async_copy(src, dst, ld.at[i]); loads[i].start()
    load(0, att_h, att); load(1, act_h, act); load(2, wout_f, woutv); load(3, wdown_f, wdownv)
    load(4, cot_h, cot); load(5, dact_h, gh); load(6, gp_h, gp); load(7, nrm_h, nrm); load(8, rows_h, rowsv)
    load(9, tok_h.at[pl.ds(pl.multiple_of(t_own * 128, 128), 128)], tok)
    def chunk(j):
        s = j % 2; r = pl.ds(j * 256, 256)
        load(10 + 2 * s, wq_f.at[:, r], wqc.at[s]); load(11 + 2 * s, wup_f.at[r], wuc.at[s])
    chunk(0); chunk(1)
    enter(peers_all())
    bs = TensorSum(brp, fa, t1a, t2a, zsa, zra, ss.at[0], rs.at[0])
    gs = TensorSum(gnp, fb, t1b, t2b, zsb, zrb, ss.at[1], rs.at[1])
    mg = TensorGather(mixed, ss.at[2], rs.at[2])
    ig = TensorGather(ingrad, ss.at[3], rs.at[3])
    s2 = Scatter(g, sib2, m2, ss.at[4], rs.at[4], 1280)
    su = Scatter(g, sibu, mu, ss.at[5], rs.at[5], 1024)
    sq = Scatter(g, sibq, mq, ss.at[6], rs.at[6], 768)
    sm = SmallSum(v, rc, rz, ry, rx, rt, acc, osv, ss.at[7], rs.at[7])

    def branch(a, b):
        ra, rb = (pl.ds(pl.multiple_of(t * 128, 128), 128) for t in (a, b))
        la = jnp.concatenate([att[ra, :], att[rb, :]], 0); lb = jnp.concatenate([act[ra, :], act[rb, :]], 0)
        def go(j, carry):
            cols = pl.ds(pl.multiple_of(j * 512, 512), 512)
            p = (NN(la, woutv[:, cols]) + NN(lb, wdownv[:, cols])).astype(bf16)
            brp[a, :, cols] = p[0:128]; brp[b, :, cols] = p[128:256]
            return carry
        lax.fori_loop(0, 4, go, 0)
    def grad_hidden():
        def go(i, carry):
            r = pl.ds(pl.multiple_of(i * 256, 256), 256)
            gr = cot[r, :]
            for j in range(2):
                cols = pl.ds(j * 512, 512)
                p = NT(gr, wdownv[cols, :])
                gh[r, cols] = (p * gh[r, cols].astype(f32)).astype(bf16)
            return carry
        lax.fori_loop(0, 4, go, 0)
    def grad_normed(j):
        s = j % 2
        loads[10 + 2 * s].wait(); loads[11 + 2 * s].wait()
        def go(i, carry):
            r = pl.ds(pl.multiple_of(i * 256, 256), 256)
            p = NT(gh[r, :], wuc[s])
            for e in range(3): p = p + NT(gp[r, e * 256:(e + 1) * 256], wqc[s, e])
            p = p.astype(bf16)
            gnp[2 * i, :, j * 256:(j + 1) * 256] = p[0:128]; gnp[2 * i + 1, :, j * 256:(j + 1) * 256] = p[128:256]
            return carry
        lax.fori_loop(0, 4, go, 0)
        if j + 2 < 8: chunk(j + 2)
    def bias_sums():
        ones = jnp.ones((16, 1024), bf16)
        for d in range(8):
            w = v.at[:, d // 4, d % 4]
            gb = NN(ones, cot[:, d * 256:(d + 1) * 256])[0:1]
            gu_ = NN(ones, gh[:, d * 128:(d + 1) * 128])[0:1]
            for cc in range(2):
                w[cc, 2:3, :] = gb[:, cc * 128:(cc + 1) * 128]; w[cc, 3:4, :] = gu_
        for j in range(3):
            gqb = NN(ones, gp[:, j * 256:(j + 1) * 256])[0:1]
            for d in range(16):
                w = v.at[d % 2, d // 8, (d // 2) % 4]
                w[4 + 2 * j:5 + 2 * j, :] = gqb[:, 0:128]; w[5 + 2 * j:6 + 2 * j, :] = gqb[:, 128:256]
    def mix(r): own[0, r, :] = (tok[r, :].astype(f32) + bs.total(r) + rowsv[2:3, :]).astype(bf16)
    def norm_back():
        sums[...] = jnp.zeros_like(sums)
        cot_own = cot.at[pl.ds(pl.multiple_of(t_own * 128, 128), 128)]
        by_rows(128, 16, lambda r: norm_back_rows(r, gs.total(r), tok, cot_own, rowsv[0:1, :], own.at[1], sums))
    def norm_sums():
        sg = jnp.sum(sums[0], axis=0, keepdims=True); sb = jnp.sum(sums[1], axis=0, keepdims=True)
        for d in range(16):
            w = v.at[d % 2, d // 8, (d // 2) % 4]
            w[0:1, :] = sg[:, d * 128:(d + 1) * 128]; w[1:2, :] = sb[:, d * 128:(d + 1) * 128]
    def put2(r, t): o2[r, :] = t
    def putu(r, t): oup[r, :] = t
    def putq(r, t): oq[r, :] = t
    xp = lambda k: (x + k) % 4
    o = 1 - zh

    for i in (0, 1, 2, 3): loads[i].wait()
    branch(o * 4 + xp(2), zh * 4 + xp(2)); bs.start_far()
    branch(o * 4 + xp(1), o * 4 + xp(3)); branch(zh * 4 + xp(1), zh * 4 + xp(3)); bs.start_near()
    branch(o * 4 + xp(0), zh * 4 + xp(0))
    loads[4].wait(); loads[5].wait()
    grad_hidden()
    s2.produce(cot, [att, act])
    bs.middle(); bs.last()
    s2.pairs(); s2.serve1()
    loads[6].wait()
    for j in range(4): grad_normed(j)
    bs.middle2()
    for j in range(4, 8): grad_normed(j)
    gs.start_far(); gs.start_near()
    s2.serve2()
    loads[7].wait()
    su.produce(nrm, [gh]); su.pairs(); su.serve1()
    sq.produce(nrm, [gp]); sq.pairs(); sq.serve1()
    s2.serve3()
    gs.middle()
    bias_sums()
    su.serve2()
    gs.last()
    loads[8].wait(); loads[9].wait()
    sq.serve2()
    gs.middle2()
    bs.arrived(); by_rows(128, 32, mix)
    load(14, own.at[0], mixed.at[t_own])
    mg.start(own.at[0])
    s2.serve4(put2); su.serve3(); sq.serve3()
    gs.arrived(); norm_back()
    load(15, own.at[1], ingrad.at[t_own])
    ig.start(own.at[1])
    norm_sums(); sm.a()
    mg.middle()
    su.serve4(putu)
    sm.b()
    sq.serve4(putq)
    sm.c_(); mg.far(); sm.d(); ig.middle(); sm.e()
    ig.far(); sm.f(); mg.finish(); ig.finish()
    loads[14].wait(); loads[15].wait()
    for w in (gs, bs, mg, ig, s2, su, sq, sm): w.drain()

def backward(wq_f, wout_f, wup_f, wdown_f, rows, nrm, att, act, dact, gp, cot, tok):
    S = jax.ShapeDtypeStruct
    vm = lambda sh, t=bf16: pltpu.VMEM(sh, t)
    tsum = [vm((128, 2048)), vm((128, 2048)), vm((2, 2, 128, 2048)), vm((128, 2048)), vm((128, 2048))]
    A = pl.BlockSpec(memory_space=pl.ANY); V = pl.BlockSpec(memory_space=pltpu.VMEM)
    return pl.pallas_call(backward_kernel,
        out_shape=[S((8, 128, 2048), bf16)] * 2 + [S((128, 1280), f32), S((128, 1024), f32), S((128, 768), f32), S((16, 128), f32)],
        in_specs=[A] * 12, out_specs=[A] * 2 + [V] * 4,
        scratch_shapes=[vm((256, 2048)), vm((1024, 2048)), vm((2, 3, 256, 256)), vm((2, 256, 1024)), vm((1024, 2048)), vm((1024, 2048)), vm((1024, 256)), vm((1024, 1024)), vm((1024, 1024)),
                        vm((1024, 768)), vm((8, 2048), f32), vm((128, 2048)), vm((8, 128, 2048)), vm((8, 128, 2048)), vm((2, 128, 2048))]
        + tsum + tsum + [vm((8, 2, 128, 1280)), vm((8, 128, 1280)), vm((7, 128, 1280)), vm((8, 128, 1024)), vm((7, 128, 1024)), vm((8, 128, 768)), vm((7, 128, 768)),
            vm((2, 2, 4, 16, 128), f32), vm((2, 4, 16, 128), f32), vm((4, 16, 128), f32), vm((3, 16, 128), f32), vm((3, 16, 128), f32), vm((16, 128), f32),
            vm((2, 16, 128), f32), vm((2, 8, 2048), f32),
            pltpu.SemaphoreType.DMA((8, 16)), pltpu.SemaphoreType.DMA((8, 16)), pltpu.SemaphoreType.DMA((16,))],
        compiler_params=pltpu.CompilerParams(collective_id=2, has_side_effects=True, vmem_limit_bytes=64 << 20),
        name="backward_and_sums")(wq_f, wout_f, wup_f, wdown_f, rows, nrm, att, act, dact, gp, cot, tok)

def hand_over_kernel(mixed, ingrad, o2, oup, oq, osv, mo, io, gg, gb, gq, gbq, go, gbo, gu, gbu, gd, gbd, big, li, lo):
    dp = lax.axis_index("dp")
    ins = [pltpu.make_async_copy((mixed, ingrad)[i // 8].at[i % 8], big.at[i], li.at[i]) for i in range(16)]
    for cp in ins: cp.start()
    gg[...] = osv[0:1, :]; gb[...] = osv[1:2, :]; gbo[...] = osv[2:3, :]; gbd[...] = osv[2:3, :]
    for j in range(3): gq[j] = oq[:, j * 256:(j + 1) * 256]
    for b in range(10):
        t = o2[:, b * 128:(b + 1) * 128].T
        if b < 2: go[b * 128:(b + 1) * 128, :] = t
        else: gd[(b - 2) * 128:(b - 1) * 128, :] = t
    gu[...] = oup[...]
    l = lax.broadcasted_iota(jnp.int32, (128, 64), 0); k = lax.broadcasted_iota(jnp.int32, (128, 64), 1)
    gbu[...] = lax.dot_general(osv[3:4, :], (l == k + 64 * (dp % 2)).astype(f32), (((1,), (0,)), ((), ())), precision=lax.Precision.HIGHEST)
    l = lax.broadcasted_iota(jnp.int32, (128, 4), 0); k = lax.broadcasted_iota(jnp.int32, (128, 4), 1)
    for j in range(3):
        rows = osv[4 + 2 * j:6 + 2 * j, :]
        lo_, hi_ = (lax.dot_general(rows, (l == k + 4 * dp + 64 * h).astype(f32), (((1,), (0,)), ((), ())), precision=lax.Precision.HIGHEST) for h in (0, 1))
        gbq[j] = jnp.concatenate([lo_[0:1], hi_[0:1], lo_[1:2], hi_[1:2]], 0)
    outs = []
    for i in range(16):
        ins[i].wait()
        cp = pltpu.make_async_copy(big.at[i], (mo, io)[i // 8].at[pl.ds((i % 8) * 128, 128)], lo.at[i]); cp.start(); outs.append(cp)
    for cp in outs: cp.wait()

def hand_over(mixed, ingrad, o2, oup, oq, osv):
    S = jax.ShapeDtypeStruct
    A = pl.BlockSpec(memory_space=pl.ANY)
    full = lambda sh: pl.BlockSpec(sh, lambda: (0,) * len(sh))
    ins = [(128, 1280), (128, 1024), (128, 768), (16, 128)]
    outs = [(1, 128), (1, 128), (3, 128, 256), (3, 4, 4), (256, 128), (1, 128), (128, 1024), (1, 64), (1024, 128), (1, 128)]
    return pl.pallas_call(hand_over_kernel,
        out_shape=[S((1024, 2048), bf16)] * 2 + [S(sh, f32) for sh in outs],
        in_specs=[A] * 2 + [full(sh) for sh in ins], out_specs=[A] * 2 + [full(sh) for sh in outs],
        scratch_shapes=[pltpu.VMEM((16, 128, 2048), bf16), pltpu.SemaphoreType.DMA((16,)), pltpu.SemaphoreType.DMA((16,))],
        compiler_params=pltpu.CompilerParams(vmem_limit_bytes=40 << 20),
        name="hand_over")(mixed, ingrad, o2, oup, oq, osv)

def body(tokens, ln_gain, ln_bias, w_qkv, b_qkv, w_out, b_out, w_up, b_up, w_down, b_down, cotangent):
    row = lambda a: a.reshape(1, 128)
    vecs, wq_f, wout_f, wup_f, wdown_f, rows, nrm, att, act, dact, gp = forward(
        (row(ln_gain), row(ln_bias), row(b_out), row(b_down), b_up, b_qkv), w_qkv.transpose(1, 0, 2), w_out, w_up, w_down,
        tokens, cotangent, jnp.asarray(rotary_tables()))
    parts = backward(wq_f, wout_f, wup_f, wdown_f, rows, nrm, att, act, dact, gp, cotangent, tokens)
    mixed, ingrad, gg, gb, gq, gbq, go, gbo, gu, gbu, gd, gbd = hand_over(*parts)
    return (mixed, ingrad, gg.reshape(128), gb.reshape(128), gq.transpose(1, 0, 2), gbq, go, gbo.reshape(128), gu, gbu, gd, gbd.reshape(128))


def solution(mesh):
    in_specs = (
        P("dp", None),
        P("dp"),
        P("dp"),
        P("dp", None, "tensor"),
        P(None, "tensor", "dp"),
        P("tensor", "dp"),
        P("dp"),
        P("dp", "tensor"),
        P("tensor", "dp"),
        P("tensor", "dp"),
        P("dp"),
        P("dp", None),
    )
    out_specs = (
        P("dp", None),
        P("dp", None),
        P("dp"),
        P("dp"),
        P("dp", None, "tensor"),
        P(None, "tensor", "dp"),
        P("tensor", "dp"),
        P("dp"),
        P("dp", "tensor"),
        P("tensor", "dp"),
        P("tensor", "dp"),
        P("dp"),
    )
    return jax.shard_map(body, mesh=mesh, in_specs=in_specs, out_specs=out_specs, check_vma=False)
```

time: 898 us -> 221 us (0.25)
  waiting for transfers between devices: 531 us -> 0 us
  Pallas kernels: 0 us -> 212 us
  blocking collectives: 171 us -> 0 us
  matrix products: 119 us -> 0 us
  other arithmetic: 36.9 us -> 0 us
  between operations: 17.4 us -> 0.88 us
    psum x1 -> x0, waiting for transfers between devices: 307 us -> none  [body(): branch_total = lax.psum(branch_terms, 'tensor')]
    reduce_scatter x4 -> x0, waiting for transfers between devices: 213 us -> none  [the longest x1 76.5 us: body(): lax.psum_scatter(grad_down, 'dp', scatter_dimension=1, tiled=True)]
    pallas_call x0 -> x3, Pallas kernels: none -> 212 us  [the longest x1 139 us: backward(): pl.pallas_call(backward_kernel, out_shape=[S((8, 128, 2048), bf16)] * 2 +...]
    dot_general x24 -> x0, matrix products: 119 us -> none  [the longest x1 13.1 us: body(): jnp.einsum('td,fd->tf', cotangent, down_back, preferred_element_type=jnp....]
    unnamed x2 -> x0, blocking collectives: 86.4 us -> none
    all_gather x5 -> x0, blocking collectives: 84.6 us -> none  [the longest x1 18.3 us: body(): lax.all_gather(b_out, 'dp', axis=0, tiled=True)]
    reduce_sum x7 -> x0, other arithmetic: 25.5 us -> none  [the longest x1 10.9 us: body(): grad_out_bias = jnp.sum(upstream_wide, axis=0)]
  transfers between devices with their start and end apart: 10 -> 0, of which waited for: 5 -> 0; matrix products, arithmetic and copies ran while one was open for 17% -> 0% of each run, Pallas kernels for 0% -> 0%
where the time goes in v1:
time: 221 us
  Pallas kernels  212 us (96%)
  local copies, waits for them, and re-layouts  8.19 us (4%)
    pallas_call x1, Pallas kernels, backward(): pl.pallas_call(backward_kernel, out_shape=[S((8, 128, 2048), bf16)] * 2 +...  139 us
    pallas_call x1, Pallas kernels, forward(): pl.pallas_call(forward_kernel, out_shape=[S((512, 128), bf16), S((3, 2048...  66.3 us
    unnamed x12, local copies, waits for them, and re-layouts  8.19 us
    pallas_call x1, Pallas kernels, hand_over(): pl.pallas_call(hand_over_kernel, out_shape=[S((1024, 2048), bf16)] * 2 +...  5.87 us

profile of v1, /device:TPU:0, one launch (start us, length us, event | category | flops | bytes accessed | tf_op | source)
XLA Modules:
  0.0 220.6 jit_solution(4086289234262154327)
XLA Ops:
  0.6 66.3 %gather_and_forward.1 = (bf16[512,128]{1,0:T(8,128)(2,1)}, bf16[3,2048,256]{2,1,0:T(8,128)(2,1)}, bf16[256,2048]{1,0:T(8,128)(2,1)}, bf16[2048,1024]{1,0:T(8,128...) custom-call(bf16[1,128]{1,0:T(2,128)(2,1)} %bitcast.11, ...), custom_call_target="tpu_custom_call" | custom-call | tf_op jit(solution)/shard_map/gather_and_forward/pallas_call | solution.py:382
  66.9 139.4 %backward_and_sums.1 = (bf16[8,128,2048]{2,1,0:T(8,128)(2,1)}, bf16[8,128,2048]{2,1,0:T(8,128)(2,1)}, f32[128,1280]{1,0:T(8,128)}, f32[128,1024]{1,0:T(8,128)}, f32[128,768]{1,0:T(8,128)}, /*index=5*/f32[16,128]{1,0:T(8,128)}) custom-call(bf16[3,2048,256]{2,1,0:T(8,128)(2,1)} %get-tuple-element.40.wq_f, bf16[256,2048]{1,0:T(8,128)(2,1)} %get-tuple-element.41.wout_f, ...), custom_call_target="tpu_custom_call" | custom-call | tf_op jit(solution)/shard_map/backward_and_sums/pallas_call | solution.py:581
  206.4 0.0 copy-start
  206.4 2.2 copy-done
  208.6 0.0 copy-start.1
  208.6 2.2 copy-done.1
  210.7 0.0 copy-start.2
  210.7 1.1 copy-done.2
  211.8 0.0 copy-start.3
  211.8 1.0 copy-done.3
  212.9 0.0 copy-start.4
  212.9 1.0 copy-done.4
  213.9 0.0 copy-start.5
  213.9 0.7 copy-done.5
  214.6 5.9 %hand_over.1 = (bf16[1024,2048]{1,0:T(8,128)(2,1)}, bf16[1024,2048]{1,0:T(8,128)(2,1)}, f32[1,128]{1,0:T(1,128)}, f32[1,128]{1,0:T(1,128)}, f32[3,128,256]{2,1,0...) custom-call(bf16[8,128,2048]{2,1,0:T(8,128)(2,1)S(1)} %copy-done, ...), custom_call_target="tpu_custom_call" | custom-call | tf_op jit(solution)/shard_map/hand_over/pallas_call | solution.py:623
Async XLA Ops:
  206.4 2.2 copy-start
  208.6 2.2 copy-start.1
  210.7 1.1 copy-start.2
  211.8 1.0 copy-start.3
  212.9 1.0 copy-start.4
  213.9 0.7 copy-start.5

commit v2 on v1

--- a/solution.py
+++ b/solution.py
@@ -119,6 +119,7 @@
     def start_near(s):
         o = 1 - s.zh
         s.send(1, s.blk(o, 1), s.t2.at[0, o], s.xu); s.send(2, s.blk(o, 3), s.t2.at[1, o], s.xd)
+    def start_near2(s):
         s.send(3, s.blk(s.zh, 1).at[s.HI], s.t2.at[0, s.zh, s.HI], s.xu); s.send(4, s.blk(s.zh, 3).at[s.LO], s.t2.at[1, s.zh, s.LO], s.xd)
     def middle(s):
         s.got(0, s.f); add_into(s.f, [s.f, s.blk(s.zh, 2)], 128, 32)
@@ -152,6 +153,7 @@
     def middle(s):
         b = s.blk(s.zh, 3); s.got(0, b); s.send(3, b.at[s.LO], b.at[s.LO], s.xu)
         b = s.blk(s.zh, 1); s.got(1, b); s.send(4, b.at[s.HI], b.at[s.HI], s.xd)
+    def plane(s):
         b = s.blk(1 - s.zh, 0); s.got(2, b); s.send(5, b, b, s.xu); s.send(6, b, b, s.xd)
     def far(s):
         b = s.blk(s.zh, 2); s.got(3, b.at[s.LO]); s.got(4, b.at[s.HI]); s.send(7, b, b, s.zf)
@@ -201,9 +203,9 @@
     ig = cot[r, :].astype(f32) + inv * (sc - jnp.mean(sc, axis=-1, keepdims=True) - xh * jnp.mean(sc * xh, axis=-1, keepdims=True))
     out[r, :] = ig.astype(bf16)
 
-PLAN = ("v0", "q0", "v1", "o0", "q1", "v2", "o1", "v3", "q2", "first", "u0", "o2", "vectors", "q3", "n0", "d0", "n1", "Aq", "n2", "u1",
-        "Wq", "n3", "sn", "o3", "p0", "p1", "p2", "p3", "Ao", "d1", "Wo", "u2", "ga", "a3x", "a3y", "a2x", "u3", "d2", "a2y", "a1x",
-        "a1y", "Au", "a0x", "a0y", "sa", "k", "sg", "Wu", "h0", "d3", "h1", "h2", "h3")
+PLAN = ("v0", "o0", "q0", "v1", "o1", "q1", "v2", "v3", "o2", "q2", "u0", "first", "o3", "vectors", "d0", "n1", "Ao", "n2", "q3", "n0",
+        "Wo", "ga", "Aq", "u1", "n3", "Wq", "sn", "p1", "p3", "p2", "p0", "d1", "u2", "a3y", "a0y", "a3x", "a1x", "u3", "a0x", "d2",
+        "a2y", "a2x", "Au", "a1y", "k", "sg", "sa", "Wu", "h2", "d3", "h1", "h0", "h3")
 
 def NT(a, b): return lax.dot_general(a, b, (((1,), (1,)), ((), ())), preferred_element_type=f32)
 def NN(a, b): return lax.dot_general(a, b, (((1,), (0,)), ((), ())), preferred_element_type=f32)
@@ -257,13 +259,13 @@
     def norm(lo, hi):
         gain, bias = rowsv[0:1, :], rowsv[1:2, :]
         def go_(i, carry):
-            r = pl.ds(pl.multiple_of(lo + i * 32, 32), 32)
+            r = pl.ds(pl.multiple_of(lo + i * 128, 128), 128)
             a = tok[r, :].astype(f32)
             cen = a - jnp.mean(a, axis=-1, keepdims=True)
             inv = lax.rsqrt(jnp.mean(cen * cen, axis=-1, keepdims=True) + norm_epsilon)
             nrm[r, :] = (cen * inv * gain + bias).astype(bf16)
             return carry
-        lax.fori_loop(0, (hi - lo) // 32, go_, 0)
+        lax.fori_loop(0, (hi - lo) // 128, go_, 0)
 
     def project(lo, hi):
         def go_(i, carry):
@@ -390,6 +392,11 @@
         compiler_params=pltpu.CompilerParams(collective_id=1, has_side_effects=True, vmem_limit_bytes=60 << 20),
         name="gather_and_forward")(*vectors, wq, wout, wup, wdown, tokens, cot, tab)
 
+PLAN_B = ("L0", "bB", "L1", "bA", "bC", "bD", "h0", "h1", "n0", "n1", "bM", "n2", "n3", "gS", "s2P0", "s2P1", "s2P2", "bL", "s2p0", "s2P3",
+          "gM", "bias", "s2p1", "bN", "s21", "suP0", "gL", "gN", "mS", "sup0", "suP1", "s22", "iS", "sup1", "sqP0", "su1", "sqP1", "va", "vb", "mM",
+          "sqp0", "vc", "sqp1", "iM", "sq1", "su2", "mP", "s23", "mF", "vd", "sq2", "iF", "su3", "iP", "sq3", "s24", "su4", "ve", "vf", "mE",
+          "sq4", "iE")
+
 class Scatter(Link):
     def __init__(s, g, sib, mid, ss, rs, width):
         super().__init__(ss, rs)
@@ -397,22 +404,19 @@
     def to_sibling(s, k):
         return pltpu.make_async_remote_copy(s.g.at[k, 1 - s.c, :, pl.ds(0, s.w)], s.b.at[k], s.ss.at[k], s.rs.at[k],
                                             device_id=s.sib, device_id_type=MESH)
-    def produce(s, lhs, rhs_list):
-        def go(k, carry):
-            chip = (k % 2) * 4 + (s.y + 2 + 3 * (k // 2)) % 4
-            a = lhs[:, pl.ds(pl.multiple_of(chip * 256, 256), 256)]
-            at = 0
-            for rhs in rhs_list:
-                n = rhs.shape[1]
-                for lo in range(0, n, 512):
-                    w = min(512, n - lo)
-                    p = TN(a, rhs[:, lo:lo + w]).astype(bf16)
-                    s.g[k, 0, :, at:at + w] = p[0:128]; s.g[k, 1, :, at:at + w] = p[128:256]
-                    at += w
-            s.to_sibling(k).start()
-            return carry
-        lax.fori_loop(0, 8, go, 0)
-    def pairs(s):
+    def produce(s, lhs, rhs, lo, hi):
+        n = rhs.shape[1]
+        def go(j, carry):
+            y = (s.y + 2 + 3 * j) % 4
+            for p in range(2):
+                a = lhs[:, pl.ds(pl.multiple_of((p * 4 + y) * 256, 256), 256)]
+                for at in range(0, n, 256):
+                    r = TN(a, rhs[:, at:at + 256]).astype(bf16)
+                    s.g[2 * j + p, 0, :, at:at + 256] = r[0:128]; s.g[2 * j + p, 1, :, at:at + 256] = r[128:256]
+                s.to_sibling(2 * j + p).start()
+            return carry
+        lax.fori_loop(lo, hi, go, 0)
+    def pairs(s, lo, hi):
         def go(k, carry):
             s.to_sibling(k).wait()
             mine = s.g.at[k, s.c]; dst = s.b.at[k]
@@ -422,7 +426,7 @@
                 return cc
             lax.fori_loop(0, 4, rows, 0)
             return carry
-        lax.fori_loop(0, 8, go, 0)
+        lax.fori_loop(lo, hi, go, 0)
     def serve1(s):
         s.send(8, s.b.at[0], s.m.at[0], s.yu); s.send(9, s.b.at[1], s.m.at[1], s.yd)
         s.send(10, s.b.at[3], s.m.at[4], s.yu); s.send(11, s.b.at[6], s.m.at[2], s.yd)
@@ -445,21 +449,19 @@
 
 def backward_kernel(wq_f, wout_f, wup_f, wdown_f, rows_h, nrm_h, att_h, act_h, dact_h, gp_h, cot_h, tok_h,
                     mixed, ingrad, o2, oup, oq, osv,
-                    woutv, wdownv, wqc, wuc, cot, nrm, att, act, gh, gp, rowsv, tok, brp, gnp, own,
+                    wb, wch, cot, nrm, aa, pq, rowsv, tok, brp, gnp, own,
                     fa, t1a, t2a, zsa, zra, fb, t1b, t2b, zsb, zrb, g, sib2, m2, sibu, mu, sibq, mq,
                     v, rc, rz, ry, rx, rt, acc, sums, ss, rs, ld):
     c, y, zl, x, zh = place()
     t_own = zh * 4 + x
+    o = 1 - zh
     loads = {}
     def load(i, src, dst):
         loads[i] = pltpu.make_async_copy(src, dst, ld.at[i]); loads[i].start()
-    load(0, att_h, att); load(1, act_h, act); load(2, wout_f, woutv); load(3, wdown_f, wdownv)
-    load(4, cot_h, cot); load(5, dact_h, gh); load(6, gp_h, gp); load(7, nrm_h, nrm); load(8, rows_h, rowsv)
-    load(9, tok_h.at[pl.ds(pl.multiple_of(t_own * 128, 128), 128)], tok)
-    def chunk(j):
-        s = j % 2; r = pl.ds(j * 256, 256)
-        load(10 + 2 * s, wq_f.at[:, r], wqc.at[s]); load(11 + 2 * s, wup_f.at[r], wuc.at[s])
-    chunk(0); chunk(1)
+    def wait(*ids):
+        for i in ids: loads[i].wait()
+    load(0, att_h, aa.at[:, pl.ds(0, 256)]); load(1, act_h, aa.at[:, pl.ds(256, 1024)])
+    load(2, wout_f, wb.at[pl.ds(0, 256)]); load(3, wdown_f, wb.at[pl.ds(256, 1024)])
     enter(peers_all())
     bs = TensorSum(brp, fa, t1a, t2a, zsa, zra, ss.at[0], rs.at[0])
     gs = TensorSum(gnp, fb, t1b, t2b, zsb, zrb, ss.at[1], rs.at[1])
@@ -469,38 +471,43 @@
     su = Scatter(g, sibu, mu, ss.at[5], rs.at[5], 1024)
     sq = Scatter(g, sibq, mq, ss.at[6], rs.at[6], 768)
     sm = SmallSum(v, rc, rz, ry, rx, rt, acc, osv, ss.at[7], rs.at[7])
-
+    gp, gh = pq.at[:, pl.ds(0, 768)], pq.at[:, pl.ds(768, 1024)]
+
+    def chunk(j):
+        s = j % 2; r = pl.ds(j * 512, 512)
+        for e in range(3): load(10 + 4 * s + e, wq_f.at[e, r], wch.at[s, :, pl.ds(e * 256, 256)])
+        load(13 + 4 * s, wup_f.at[r], wch.at[s, :, pl.ds(768, 1024)])
+    def first_loads(): wait(0, 1, 2, 3)
+    def other_loads():
+        load(4, cot_h, cot); load(5, dact_h, gh); load(6, gp_h, gp); chunk(0); chunk(1); load(7, nrm_h, nrm)
+        load(8, rows_h, rowsv); load(9, tok_h.at[pl.ds(pl.multiple_of(t_own * 128, 128), 128)], tok)
     def branch(a, b):
         ra, rb = (pl.ds(pl.multiple_of(t * 128, 128), 128) for t in (a, b))
-        la = jnp.concatenate([att[ra, :], att[rb, :]], 0); lb = jnp.concatenate([act[ra, :], act[rb, :]], 0)
+        lhs = jnp.concatenate([aa[ra, :], aa[rb, :]], 0)
         def go(j, carry):
             cols = pl.ds(pl.multiple_of(j * 512, 512), 512)
-            p = (NN(la, woutv[:, cols]) + NN(lb, wdownv[:, cols])).astype(bf16)
+            p = NN(lhs, wb[:, cols]).astype(bf16)
             brp[a, :, cols] = p[0:128]; brp[b, :, cols] = p[128:256]
             return carry
         lax.fori_loop(0, 4, go, 0)
-    def grad_hidden():
+    def grad_hidden(lo, hi):
+        if lo == 0: wait(4, 5)
         def go(i, carry):
-            r = pl.ds(pl.multiple_of(i * 256, 256), 256)
+            r = pl.ds(pl.multiple_of(i * 512, 512), 512)
             gr = cot[r, :]
-            for j in range(2):
-                cols = pl.ds(j * 512, 512)
-                p = NT(gr, wdownv[cols, :])
-                gh[r, cols] = (p * gh[r, cols].astype(f32)).astype(bf16)
-            return carry
-        lax.fori_loop(0, 4, go, 0)
+            for j in range(4):
+                p = NT(gr, wb[256 + j * 256:512 + j * 256, :])
+                cols = pl.ds(768 + j * 256, 256)
+                pq[r, cols] = (p * pq[r, cols].astype(f32)).astype(bf16)
+            return carry
+        lax.fori_loop(lo, hi, go, 0)
     def grad_normed(j):
         s = j % 2
-        loads[10 + 2 * s].wait(); loads[11 + 2 * s].wait()
-        def go(i, carry):
-            r = pl.ds(pl.multiple_of(i * 256, 256), 256)
-            p = NT(gh[r, :], wuc[s])
-            for e in range(3): p = p + NT(gp[r, e * 256:(e + 1) * 256], wqc[s, e])
-            p = p.astype(bf16)
-            gnp[2 * i, :, j * 256:(j + 1) * 256] = p[0:128]; gnp[2 * i + 1, :, j * 256:(j + 1) * 256] = p[128:256]
-            return carry
-        lax.fori_loop(0, 4, go, 0)
-        if j + 2 < 8: chunk(j + 2)
+        if j == 0: wait(6)
+        wait(*range(10 + 4 * s, 14 + 4 * s))
+        p = NT(pq[...], wch[s]).astype(bf16)
+        gnp[:, :, j * 512:(j + 1) * 512] = p.reshape(8, 128, 512)
+        if j + 2 < 4: chunk(j + 2)
     def bias_sums():
         ones = jnp.ones((16, 1024), bf16)
         for d in range(8):
@@ -514,63 +521,52 @@
             for d in range(16):
                 w = v.at[d % 2, d // 8, (d // 2) % 4]
                 w[4 + 2 * j:5 + 2 * j, :] = gqb[:, 0:128]; w[5 + 2 * j:6 + 2 * j, :] = gqb[:, 128:256]
-    def mix(r): own[0, r, :] = (tok[r, :].astype(f32) + bs.total(r) + rowsv[2:3, :]).astype(bf16)
-    def norm_back():
+    def mixed_start():
+        bs.arrived()
+        def mix(r): own[0, r, :] = (tok[r, :].astype(f32) + bs.total(r) + rowsv[2:3, :]).astype(bf16)
+        wait(8, 9)
+        by_rows(128, 64, mix)
+        load(18, own.at[0], mixed.at[t_own])
+        mg.start(own.at[0])
+    def ingrad_start():
+        gs.arrived()
         sums[...] = jnp.zeros_like(sums)
         cot_own = cot.at[pl.ds(pl.multiple_of(t_own * 128, 128), 128)]
-        by_rows(128, 16, lambda r: norm_back_rows(r, gs.total(r), tok, cot_own, rowsv[0:1, :], own.at[1], sums))
+        by_rows(128, 32, lambda r: norm_back_rows(r, gs.total(r), tok, cot_own, rowsv[0:1, :], own.at[1], sums))
+        load(19, own.at[1], ingrad.at[t_own])
+        ig.start(own.at[1])
     def norm_sums():
         sg = jnp.sum(sums[0], axis=0, keepdims=True); sb = jnp.sum(sums[1], axis=0, keepdims=True)
         for d in range(16):
             w = v.at[d % 2, d // 8, (d // 2) % 4]
             w[0:1, :] = sg[:, d * 128:(d + 1) * 128]; w[1:2, :] = sb[:, d * 128:(d + 1) * 128]
+        sm.a()
     def put2(r, t): o2[r, :] = t
     def putu(r, t): oup[r, :] = t
     def putq(r, t): oq[r, :] = t
-    xp = lambda k: (x + k) % 4
-    o = 1 - zh
-
-    for i in (0, 1, 2, 3): loads[i].wait()
-    branch(o * 4 + xp(2), zh * 4 + xp(2)); bs.start_far()
-    branch(o * 4 + xp(1), o * 4 + xp(3)); branch(zh * 4 + xp(1), zh * 4 + xp(3)); bs.start_near()
-    branch(o * 4 + xp(0), zh * 4 + xp(0))
-    loads[4].wait(); loads[5].wait()
-    grad_hidden()
-    s2.produce(cot, [att, act])
-    bs.middle(); bs.last()
-    s2.pairs(); s2.serve1()
-    loads[6].wait()
-    for j in range(4): grad_normed(j)
-    bs.middle2()
-    for j in range(4, 8): grad_normed(j)
-    gs.start_far(); gs.start_near()
-    s2.serve2()
-    loads[7].wait()
-    su.produce(nrm, [gh]); su.pairs(); su.serve1()
-    sq.produce(nrm, [gp]); sq.pairs(); sq.serve1()
-    s2.serve3()
-    gs.middle()
-    bias_sums()
-    su.serve2()
-    gs.last()
-    loads[8].wait(); loads[9].wait()
-    sq.serve2()
-    gs.middle2()
-    bs.arrived(); by_rows(128, 32, mix)
-    load(14, own.at[0], mixed.at[t_own])
-    mg.start(own.at[0])
-    s2.serve4(put2); su.serve3(); sq.serve3()
-    gs.arrived(); norm_back()
-    load(15, own.at[1], ingrad.at[t_own])
-    ig.start(own.at[1])
-    norm_sums(); sm.a()
-    mg.middle()
-    su.serve4(putu)
-    sm.b()
-    sq.serve4(putq)
-    sm.c_(); mg.far(); sm.d(); ig.middle(); sm.e()
-    ig.far(); sm.f(); mg.finish(); ig.finish()
-    loads[14].wait(); loads[15].wait()
+    def xp(k): return (x + k) % 4
+    def far(): branch(o * 4 + xp(2), zh * 4 + xp(2)); bs.start_far()
+    def near(): branch(o * 4 + xp(1), o * 4 + xp(3)); bs.start_near()
+    def near2(): branch(zh * 4 + xp(1), zh * 4 + xp(3)); bs.start_near2()
+    def home(): branch(o * 4 + xp(0), zh * 4 + xp(0))
+    def gn_start(): gs.start_far(); gs.start_near(); gs.start_near2()
+    steps = {"L0": first_loads, "L1": other_loads, "bA": far, "bB": near, "bC": near2, "bD": home, "gS": gn_start, "bias": bias_sums,
+             "mS": mixed_start, "iS": ingrad_start, "va": norm_sums, "vb": sm.b, "vc": sm.c_, "vd": sm.d, "ve": sm.e, "vf": sm.f,
+             "h0": partial(grad_hidden, 0, 1), "h1": partial(grad_hidden, 1, 2),
+             "s24": partial(s2.serve4, put2), "su4": partial(su.serve4, putu), "sq4": partial(sq.serve4, putq)}
+    for i in range(4):
+        steps["n%d" % i] = partial(grad_normed, i); steps["s2P%d" % i] = partial(s2.produce, cot, aa, i, i + 1)
+    def up_grads(lo, hi):
+        if lo == 0: wait(7)
+        su.produce(nrm, gh, lo, hi)
+    for i in range(2):
+        steps["suP%d" % i] = partial(up_grads, 2 * i, 2 * i + 2); steps["sqP%d" % i] = partial(sq.produce, nrm, gp, 2 * i, 2 * i + 2)
+        for nm, w in (("s2", s2), ("su", su), ("sq", sq)): steps[nm + "p%d" % i] = partial(w.pairs, 4 * i, 4 * i + 4)
+    for nm, w in (("s2", s2), ("su", su), ("sq", sq)): steps[nm + "1"], steps[nm + "2"], steps[nm + "3"] = w.serve1, w.serve2, w.serve3
+    for nm, w in (("b", bs), ("g", gs)): steps[nm + "M"], steps[nm + "N"], steps[nm + "L"] = w.middle, w.middle2, w.last
+    for nm, w in (("m", mg), ("i", ig)): steps[nm + "M"], steps[nm + "P"], steps[nm + "F"], steps[nm + "E"] = w.middle, w.plane, w.far, w.finish
+    for name in PLAN_B: steps[name]()
+    wait(18, 19)
     for w in (gs, bs, mg, ig, s2, su, sq, sm): w.drain()
 
 def backward(wq_f, wout_f, wup_f, wdown_f, rows, nrm, att, act, dact, gp, cot, tok):
@@ -581,26 +577,43 @@
     return pl.pallas_call(backward_kernel,
         out_shape=[S((8, 128, 2048), bf16)] * 2 + [S((128, 1280), f32), S((128, 1024), f32), S((128, 768), f32), S((16, 128), f32)],
         in_specs=[A] * 12, out_specs=[A] * 2 + [V] * 4,
-        scratch_shapes=[vm((256, 2048)), vm((1024, 2048)), vm((2, 3, 256, 256)), vm((2, 256, 1024)), vm((1024, 2048)), vm((1024, 2048)), vm((1024, 256)), vm((1024, 1024)), vm((1024, 1024)),
-                        vm((1024, 768)), vm((8, 2048), f32), vm((128, 2048)), vm((8, 128, 2048)), vm((8, 128, 2048)), vm((2, 128, 2048))]
+        scratch_shapes=[vm((1280, 2048)), vm((2, 512, 1792)), vm((1024, 2048)), vm((1024, 2048)), vm((1024, 1280)), vm((1024, 1792)),
+                        vm((8, 2048), f32), vm((128, 2048)), vm((8, 128, 2048)), vm((8, 128, 2048)), vm((2, 128, 2048))]
         + tsum + tsum + [vm((8, 2, 128, 1280)), vm((8, 128, 1280)), vm((7, 128, 1280)), vm((8, 128, 1024)), vm((7, 128, 1024)), vm((8, 128, 768)), vm((7, 128, 768)),
             vm((2, 2, 4, 16, 128), f32), vm((2, 4, 16, 128), f32), vm((4, 16, 128), f32), vm((3, 16, 128), f32), vm((3, 16, 128), f32), vm((16, 128), f32),
             vm((2, 16, 128), f32), vm((2, 8, 2048), f32),
-            pltpu.SemaphoreType.DMA((8, 16)), pltpu.SemaphoreType.DMA((8, 16)), pltpu.SemaphoreType.DMA((16,))],
+            pltpu.SemaphoreType.DMA((8, 16)), pltpu.SemaphoreType.DMA((8, 16)), pltpu.SemaphoreType.DMA((20,))],
         compiler_params=pltpu.CompilerParams(collective_id=2, has_side_effects=True, vmem_limit_bytes=64 << 20),
         name="backward_and_sums")(wq_f, wout_f, wup_f, wdown_f, rows, nrm, att, act, dact, gp, cot, tok)
 
-def hand_over_kernel(mixed, ingrad, o2, oup, oq, osv, mo, io, gg, gb, gq, gbq, go, gbo, gu, gbu, gd, gbd, big, li, lo):
+def hand_over_kernel(mixed, ingrad, o2_h, oup_h, oq_h, osv, mo, io, gg, gb, gq_h, gbq, go_h, gbo, gu_h, gbu, gd_h, gbd,
+                     big, o2, oup, oq, gq, go, gd, li, lo):
     dp = lax.axis_index("dp")
-    ins = [pltpu.make_async_copy((mixed, ingrad)[i // 8].at[i % 8], big.at[i], li.at[i]) for i in range(16)]
-    for cp in ins: cp.start()
-    gg[...] = osv[0:1, :]; gb[...] = osv[1:2, :]; gbo[...] = osv[2:3, :]; gbd[...] = osv[2:3, :]
-    for j in range(3): gq[j] = oq[:, j * 256:(j + 1) * 256]
+    def copy(a, b, sem):
+        cp = pltpu.make_async_copy(a, b, sem); cp.start()
+        return cp
+    n = 8
+    ins = [copy((mixed, ingrad)[i // 4].at[pl.ds((i % 4) * 2, 2)], big.at[i], li.at[i]) for i in range(4)]
+    small = [copy(o2_h, o2, li.at[n]), copy(oup_h, oup, li.at[n + 1]), copy(oq_h, oq, li.at[n + 2])]
+    ins += [copy((mixed, ingrad)[i // 4].at[pl.ds((i % 4) * 2, 2)], big.at[i], li.at[i]) for i in range(4, 8)]
+    outs = []
+    def pass_on(i):
+        ins[i].wait()
+        for h in range(2): outs.append(copy(big.at[i, h], (mo, io)[i // 4].at[pl.ds((i % 4) * 256 + h * 128, 128)], lo.at[2 * i + h]))
+    pass_on(0); pass_on(1)
+    small[0].wait()
     for b in range(10):
         t = o2[:, b * 128:(b + 1) * 128].T
         if b < 2: go[b * 128:(b + 1) * 128, :] = t
         else: gd[(b - 2) * 128:(b - 1) * 128, :] = t
-    gu[...] = oup[...]
+    outs += [copy(go, go_h, lo.at[16]), copy(gd, gd_h, lo.at[17])]
+    pass_on(2); pass_on(3)
+    small[1].wait(); outs.append(copy(oup, gu_h, lo.at[18]))
+    small[2].wait()
+    for j in range(3): gq[j] = oq[:, j * 256:(j + 1) * 256]
+    outs.append(copy(gq, gq_h, lo.at[19]))
+    pass_on(4); pass_on(5)
+    gg[...] = osv[0:1, :]; gb[...] = osv[1:2, :]; gbo[...] = osv[2:3, :]; gbd[...] = osv[2:3, :]
     l = lax.broadcasted_iota(jnp.int32, (128, 64), 0); k = lax.broadcasted_iota(jnp.int32, (128, 64), 1)
     gbu[...] = lax.dot_general(osv[3:4, :], (l == k + 64 * (dp % 2)).astype(f32), (((1,), (0,)), ((), ())), precision=lax.Precision.HIGHEST)
     l = lax.broadcasted_iota(jnp.int32, (128, 4), 0); k = lax.broadcasted_iota(jnp.int32, (128, 4), 1)
@@ -608,23 +621,21 @@
         rows = osv[4 + 2 * j:6 + 2 * j, :]
         lo_, hi_ = (lax.dot_general(rows, (l == k + 4 * dp + 64 * h).astype(f32), (((1,), (0,)), ((), ())), precision=lax.Precision.HIGHEST) for h in (0, 1))
         gbq[j] = jnp.concatenate([lo_[0:1], hi_[0:1], lo_[1:2], hi_[1:2]], 0)
-    outs = []
-    for i in range(16):
-        ins[i].wait()
-        cp = pltpu.make_async_copy(big.at[i], (mo, io)[i // 8].at[pl.ds((i % 8) * 128, 128)], lo.at[i]); cp.start(); outs.append(cp)
+    pass_on(6); pass_on(7)
     for cp in outs: cp.wait()
 
 def hand_over(mixed, ingrad, o2, oup, oq, osv):
     S = jax.ShapeDtypeStruct
-    A = pl.BlockSpec(memory_space=pl.ANY)
+    A = pl.BlockSpec(memory_space=pltpu.HBM)
     full = lambda sh: pl.BlockSpec(sh, lambda: (0,) * len(sh))
-    ins = [(128, 1280), (128, 1024), (128, 768), (16, 128)]
-    outs = [(1, 128), (1, 128), (3, 128, 256), (3, 4, 4), (256, 128), (1, 128), (128, 1024), (1, 64), (1024, 128), (1, 128)]
+    outs = [((1, 128), 0), ((1, 128), 0), ((3, 128, 256), 1), ((3, 4, 4), 0), ((256, 128), 1), ((1, 128), 0), ((128, 1024), 1), ((1, 64), 0), ((1024, 128), 1), ((1, 128), 0)]
+    vm = lambda sh: pltpu.VMEM(sh, f32)
     return pl.pallas_call(hand_over_kernel,
-        out_shape=[S((1024, 2048), bf16)] * 2 + [S(sh, f32) for sh in outs],
-        in_specs=[A] * 2 + [full(sh) for sh in ins], out_specs=[A] * 2 + [full(sh) for sh in outs],
-        scratch_shapes=[pltpu.VMEM((16, 128, 2048), bf16), pltpu.SemaphoreType.DMA((16,)), pltpu.SemaphoreType.DMA((16,))],
-        compiler_params=pltpu.CompilerParams(vmem_limit_bytes=40 << 20),
+        out_shape=[S((1024, 2048), bf16)] * 2 + [S(sh, f32) for sh, _ in outs],
+        in_specs=[A] * 5 + [full((16, 128))], out_specs=[A] * 2 + [A if m else full(sh) for sh, m in outs],
+        scratch_shapes=[pltpu.VMEM((8, 2, 128, 2048), bf16), vm((128, 1280)), vm((128, 1024)), vm((128, 768)), vm((3, 128, 256)), vm((256, 128)), vm((1024, 128)),
+                        pltpu.SemaphoreType.DMA((12,)), pltpu.SemaphoreType.DMA((20,))],
+        compiler_params=pltpu.CompilerParams(vmem_limit_bytes=62 << 20),
         name="hand_over")(mixed, ingrad, o2, oup, oq, osv)
 
 def body(tokens, ln_gain, ln_bias, w_qkv, b_qkv, w_out, b_out, w_up, b_up, w_down, b_down, cotangent):

time: 221 us -> 209 us (0.946); the launches traced: 221 us -> 206 us
  local copies, waits for them, and re-layouts: 8.19 us -> 0 us
  Pallas kernels: 212 us -> 205 us
    unnamed x12 -> x0, local copies, waits for them, and re-layouts: 8.19 us -> none
    pallas_call x1, Pallas kernels: 139 us -> 133 us  [backward(): pl.pallas_call(backward_kernel, out_shape=[S((8, 128, 2048), bf16)] * 2 +...]
    pallas_call x1, Pallas kernels: 5.87 us -> 8.66 us  [hand_over(): pl.pallas_call(hand_over_kernel, out_shape=[S((1024, 2048), bf16)] * 2 +...]
    pallas_call x1, Pallas kernels: 66.3 us -> 63.6 us  [forward(): pl.pallas_call(forward_kernel, out_shape=[S((512, 128), bf16), S((3, 2048...]
where the time goes in v2:
time: 209 us; the launch traced here: 206 us
  Pallas kernels  205 us (98%)
    pallas_call x1, Pallas kernels, backward(): pl.pallas_call(backward_kernel, out_shape=[S((8, 128, 2048), bf16)] * 2 +...  133 us
    pallas_call x1, Pallas kernels, forward(): pl.pallas_call(forward_kernel, out_shape=[S((512, 128), bf16), S((3, 2048...  63.6 us
    pallas_call x1, Pallas kernels, hand_over(): pl.pallas_call(hand_over_kernel, out_shape=[S((1024, 2048), bf16)] * 2 +...  8.66 us

profile of v2, /device:TPU:0, one launch (start us, length us, event | category | flops | bytes accessed | tf_op | source)
XLA Modules:
  0.0 206.3 jit_solution(16724013551323771624)
XLA Ops:
  0.6 63.6 %gather_and_forward.1 = (bf16[512,128]{1,0:T(8,128)(2,1)}, bf16[3,2048,256]{2,1,0:T(8,128)(2,1)}, bf16[256,2048]{1,0:T(8,128)(2,1)}, bf16[2048,1024]{1,0:T(8,128...) custom-call(bf16[1,128]{1,0:T(2,128)(2,1)} %bitcast.11, ...), custom_call_target="tpu_custom_call" | custom-call | tf_op jit(solution)/shard_map/gather_and_forward/pallas_call | solution.py:384
  64.3 133.2 %backward_and_sums.1 = (bf16[8,128,2048]{2,1,0:T(8,128)(2,1)}, bf16[8,128,2048]{2,1,0:T(8,128)(2,1)}, f32[128,1280]{1,0:T(8,128)}, f32[128,1024]{1,0:T(8,128)}, f32[128,768]{1,0:T(8,128)}, /*index=5*/f32[16,128]{1,0:T(8,128)}) custom-call(bf16[3,2048,256]{2,1,0:T(8,128)(2,1)} %get-tuple-element.40.wq_f, bf16[256,2048]{1,0:T(8,128)(2,1)} %get-tuple-element.41.wout_f, ...), custom_call_target="tpu_custom_call" | custom-call | tf_op jit(solution)/shard_map/backward_and_sums/pallas_call | solution.py:577
  197.5 8.7 %hand_over.1 = (bf16[1024,2048]{1,0:T(8,128)(2,1)}, bf16[1024,2048]{1,0:T(8,128)(2,1)}, f32[1,128]{1,0:T(1,128)}, f32[1,128]{1,0:T(1,128)}, f32[3,128,256]{2,1,0...) custom-call(bf16[8,128,2048]{2,1,0:T(8,128)(2,1)} %get-tuple-element, ...), custom_call_target="tpu_custom_call" | custom-call | tf_op jit(solution)/shard_map/hand_over/pallas_call | solution.py:633

commit v3 on v2

--- a/solution.py
+++ b/solution.py
@@ -203,9 +203,9 @@
     ig = cot[r, :].astype(f32) + inv * (sc - jnp.mean(sc, axis=-1, keepdims=True) - xh * jnp.mean(sc * xh, axis=-1, keepdims=True))
     out[r, :] = ig.astype(bf16)
 
-PLAN = ("v0", "o0", "q0", "v1", "o1", "q1", "v2", "v3", "o2", "q2", "u0", "first", "o3", "vectors", "d0", "n1", "Ao", "n2", "q3", "n0",
-        "Wo", "ga", "Aq", "u1", "n3", "Wq", "sn", "p1", "p3", "p2", "p0", "d1", "u2", "a3y", "a0y", "a3x", "a1x", "u3", "a0x", "d2",
-        "a2y", "a2x", "Au", "a1y", "k", "sg", "sa", "Wu", "h2", "d3", "h1", "h0", "h3")
+PLAN = ("o0", "v0", "q0", "v1", "o1", "q1", "o2", "v2", "q2", "v3", "o3", "u0", "first", "vectors", "n0", "Ao", "q3", "d0", "n1", "n2",
+        "n3", "Wo", "Aq", "u1", "ga", "Wq", "p0", "p3", "p1", "p2", "d1", "u2", "a3x", "a0x", "a3y", "sn", "a1x", "u3", "a0y", "d2",
+        "a2x", "a2y", "Au", "a1y", "k", "Wu", "h1", "d3", "sa", "sg", "h2", "h0", "h3")
 
 def NT(a, b): return lax.dot_general(a, b, (((1,), (1,)), ((), ())), preferred_element_type=f32)
 def NN(a, b): return lax.dot_general(a, b, (((1,), (0,)), ((), ())), preferred_element_type=f32)
@@ -281,11 +281,11 @@
 
     def grad_attended():
         def go_(i, carry):
-            r = pl.ds(pl.multiple_of(i * 256, 256), 256)
+            r = pl.ds(pl.multiple_of(i * 512, 512), 512)
             p = NT(cot[r, :], woutv[...])
             ga[0, r, :] = p[:, 0:128].astype(bf16); ga[1, r, :] = p[:, 128:256].astype(bf16)
             return carry
-        lax.fori_loop(0, 4, go_, 0)
+        lax.fori_loop(0, 2, go_, 0)
 
     def attention(i):
         lax.fori_loop(0, 2, lambda p, carry: attention_pair(i, p, carry), 0)
@@ -332,11 +332,14 @@
                 cols = pl.ds(j * 256, 256)
                 h = NN(n, wupv[:, cols]) + bup[0:1, cols]
                 h2 = h * h
-                t = jnp.tanh(0.7978845608028654 * h * (1.0 + 0.044715 * h2))
-                act[r, cols] = (0.5 * h * (1.0 + t)).astype(bf16)
-                dact[r, cols] = (0.5 * (1.0 + t) + 0.5 * h * (1.0 - t * t) * (0.7978845608028654 * (1.0 + 0.134145 * h2))).astype(bf16)
+                t = 0.5 + 0.5 * jnp.tanh(h * (0.7978845608028654 + 0.035677408136300125 * h2))
+                y_ = h * t
+                act[r, cols] = y_.astype(bf16)
+                dact[r, cols] = (t + y_ * ((2.0 - 2.0 * t) * (0.7978845608028654 + 0.10703222440890037 * h2))).astype(bf16)
             return carry
         lax.fori_loop(0, (hi - lo) // 256, go_, 0)
+        r = pl.ds(lo, hi - lo)
+        load(13 + lo // 256, act.at[r], act_h.at[r]); load(17 + lo // 256, dact.at[r], dact_h.at[r])
 
     def first():
         gv.arrived(); local[0].wait(); load(2, vecs, vv)
@@ -370,9 +373,8 @@
     for nm, g in (("v", gv), ("q", gq), ("o", go), ("u", gu), ("d", gd)):
         steps[nm + "0"], steps[nm + "1"], steps[nm + "2"], steps[nm + "3"] = g.start, g.serve, g.serve2, g.serve3
     for name in PLAN: steps[name]()
-    load(10, act, act_h); load(11, dact, dact_h)
     gd.arrived()
-    for i in (5, 6, 8, 9, 10, 11): loads[i].wait()
+    for i in (5, 6, 8, 9, *range(13, 21)): loads[i].wait()
     local[4].wait()
     for g in (gv, gq, go, gu, gd):
         for cp in g.sends: cp.wait_send()
@@ -388,13 +390,13 @@
         scratch_shapes=[vm((32, 128)), vm((3, 1024, 128), f32), vm((512, 128)), vm((3, 2048, 256)), vm((256, 2048)), vm((2048, 1024)), vm((1024, 2048)), vm((1024, 2048)), vm((1024, 2048)),
                         vm((8, 2048), f32), vm((8, 128), f32), vm((8, 1024), f32), vm((2, 1024, 128)), vm((2, 1024, 128)), vm((2, 1024, 128)), vm((2, 1024, 128)),
                         vm((1024, 256)), vm((2, 1024, 128), f32), vm((2, 1024, 128), f32), vm((1024, 768)), vm((1024, 1024)), vm((1024, 1024)),
-                        pltpu.SemaphoreType.DMA((5, 16)), pltpu.SemaphoreType.DMA((5, 16)), pltpu.SemaphoreType.DMA((5,)), pltpu.SemaphoreType.DMA((13,))],
+                        pltpu.SemaphoreType.DMA((5, 16)), pltpu.SemaphoreType.DMA((5, 16)), pltpu.SemaphoreType.DMA((5,)), pltpu.SemaphoreType.DMA((21,))],
         compiler_params=pltpu.CompilerParams(collective_id=1, has_side_effects=True, vmem_limit_bytes=60 << 20),
         name="gather_and_forward")(*vectors, wq, wout, wup, wdown, tokens, cot, tab)
 
-PLAN_B = ("L0", "bB", "L1", "bA", "bC", "bD", "h0", "h1", "n0", "n1", "bM", "n2", "n3", "gS", "s2P0", "s2P1", "s2P2", "bL", "s2p0", "s2P3",
-          "gM", "bias", "s2p1", "bN", "s21", "suP0", "gL", "gN", "mS", "sup0", "suP1", "s22", "iS", "sup1", "sqP0", "su1", "sqP1", "va", "vb", "mM",
-          "sqp0", "vc", "sqp1", "iM", "sq1", "su2", "mP", "s23", "mF", "vd", "sq2", "iF", "su3", "iP", "sq3", "s24", "su4", "ve", "vf", "mE",
+PLAN_B = ("L0", "bB", "L1", "bA", "bD", "bC", "h0", "h1", "n0", "n1", "bM", "n2", "n3", "gS", "s2P0", "s2P1", "bL", "s2P2", "s2p0", "s2P3",
+          "gM", "bN", "s2p1", "s21", "gL", "suP0", "gN", "s22", "mS", "suP1", "bias", "iS", "sup0", "sup1", "su1", "sqP0", "s23", "va", "vb", "mM",
+          "sqP1", "vc", "su2", "sqp0", "iM", "sqp1", "mP", "vd", "mF", "sq1", "sq2", "su3", "iP", "s24", "iF", "ve", "mE", "sq3", "su4", "vf",
           "sq4", "iE")
 
 class Scatter(Link):
@@ -408,11 +410,12 @@
         n = rhs.shape[1]
         def go(j, carry):
             y = (s.y + 2 + 3 * j) % 4
+            a = jnp.concatenate([lhs[:, pl.ds(pl.multiple_of((p * 4 + y) * 256, 256), 256)] for p in range(2)], 1)
+            for at in range(0, n, 256):
+                r = TN(a, rhs[:, at:at + 256]).astype(bf16)
+                for p in range(2):
+                    for cc in range(2): s.g[2 * j + p, cc, :, at:at + 256] = r[p * 256 + cc * 128:p * 256 + cc * 128 + 128]
             for p in range(2):
-                a = lhs[:, pl.ds(pl.multiple_of((p * 4 + y) * 256, 256), 256)]
-                for at in range(0, n, 256):
-                    r = TN(a, rhs[:, at:at + 256]).astype(bf16)
-                    s.g[2 * j + p, 0, :, at:at + 256] = r[0:128]; s.g[2 * j + p, 1, :, at:at + 256] = r[128:256]
                 s.to_sibling(2 * j + p).start()
             return carry
         lax.fori_loop(lo, hi, go, 0)
@@ -461,7 +464,9 @@
     def wait(*ids):
         for i in ids: loads[i].wait()
     load(0, att_h, aa.at[:, pl.ds(0, 256)]); load(1, act_h, aa.at[:, pl.ds(256, 1024)])
-    load(2, wout_f, wb.at[pl.ds(0, 256)]); load(3, wdown_f, wb.at[pl.ds(256, 1024)])
+    for j in range(4):
+        cols = pl.ds(j * 512, 512)
+        load(20 + j, wout_f.at[:, cols], wb.at[pl.ds(0, 256), cols]); load(24 + j, wdown_f.at[:, cols], wb.at[pl.ds(256, 1024), cols])
     enter(peers_all())
     bs = TensorSum(brp, fa, t1a, t2a, zsa, zra, ss.at[0], rs.at[0])
     gs = TensorSum(gnp, fb, t1b, t2b, zsb, zrb, ss.at[1], rs.at[1])
@@ -477,19 +482,18 @@
         s = j % 2; r = pl.ds(j * 512, 512)
         for e in range(3): load(10 + 4 * s + e, wq_f.at[e, r], wch.at[s, :, pl.ds(e * 256, 256)])
         load(13 + 4 * s, wup_f.at[r], wch.at[s, :, pl.ds(768, 1024)])
-    def first_loads(): wait(0, 1, 2, 3)
+    def first_loads(): wait(0, 1)
     def other_loads():
         load(4, cot_h, cot); load(5, dact_h, gh); load(6, gp_h, gp); chunk(0); chunk(1); load(7, nrm_h, nrm)
         load(8, rows_h, rowsv); load(9, tok_h.at[pl.ds(pl.multiple_of(t_own * 128, 128), 128)], tok)
-    def branch(a, b):
+    def branch(a, b, first=False):
         ra, rb = (pl.ds(pl.multiple_of(t * 128, 128), 128) for t in (a, b))
         lhs = jnp.concatenate([aa[ra, :], aa[rb, :]], 0)
-        def go(j, carry):
-            cols = pl.ds(pl.multiple_of(j * 512, 512), 512)
+        for j in range(4):
+            if first: wait(20 + j, 24 + j)
+            cols = pl.ds(j * 512, 512)
             p = NN(lhs, wb[:, cols]).astype(bf16)
             brp[a, :, cols] = p[0:128]; brp[b, :, cols] = p[128:256]
-            return carry
-        lax.fori_loop(0, 4, go, 0)
     def grad_hidden(lo, hi):
         if lo == 0: wait(4, 5)
         def go(i, carry):
@@ -546,7 +550,7 @@
     def putq(r, t): oq[r, :] = t
     def xp(k): return (x + k) % 4
     def far(): branch(o * 4 + xp(2), zh * 4 + xp(2)); bs.start_far()
-    def near(): branch(o * 4 + xp(1), o * 4 + xp(3)); bs.start_near()
+    def near(): branch(o * 4 + xp(1), o * 4 + xp(3), True); bs.start_near()
     def near2(): branch(zh * 4 + xp(1), zh * 4 + xp(3)); bs.start_near2()
     def home(): branch(o * 4 + xp(0), zh * 4 + xp(0))
     def gn_start(): gs.start_far(); gs.start_near(); gs.start_near2()
@@ -582,7 +586,7 @@
         + tsum + tsum + [vm((8, 2, 128, 1280)), vm((8, 128, 1280)), vm((7, 128, 1280)), vm((8, 128, 1024)), vm((7, 128, 1024)), vm((8, 128, 768)), vm((7, 128, 768)),
             vm((2, 2, 4, 16, 128), f32), vm((2, 4, 16, 128), f32), vm((4, 16, 128), f32), vm((3, 16, 128), f32), vm((3, 16, 128), f32), vm((16, 128), f32),
             vm((2, 16, 128), f32), vm((2, 8, 2048), f32),
-            pltpu.SemaphoreType.DMA((8, 16)), pltpu.SemaphoreType.DMA((8, 16)), pltpu.SemaphoreType.DMA((20,))],
+            pltpu.SemaphoreType.DMA((8, 16)), pltpu.SemaphoreType.DMA((8, 16)), pltpu.SemaphoreType.DMA((28,))],
         compiler_params=pltpu.CompilerParams(collective_id=2, has_side_effects=True, vmem_limit_bytes=64 << 20),
         name="backward_and_sums")(wq_f, wout_f, wup_f, wdown_f, rows, nrm, att, act, dact, gp, cot, tok)
 

time: 209 us -> 203 us (0.971)
  Pallas kernels: 205 us -> 199 us
    pallas_call x1, Pallas kernels: 133 us -> 128 us  [backward(): pl.pallas_call(backward_kernel, out_shape=[S((8, 128, 2048), bf16)] * 2 +...]
where the time goes in v3:
time: 203 us; the launch traced here: 200 us
  Pallas kernels  199 us (98%)
    pallas_call x1, Pallas kernels, backward(): pl.pallas_call(backward_kernel, out_shape=[S((8, 128, 2048), bf16)] * 2 +...  128 us
    pallas_call x1, Pallas kernels, forward(): pl.pallas_call(forward_kernel, out_shape=[S((512, 128), bf16), S((3, 2048...  62.6 us
    pallas_call x1, Pallas kernels, hand_over(): pl.pallas_call(hand_over_kernel, out_shape=[S((1024, 2048), bf16)] * 2 +...  8.66 us

profile of v3, /device:TPU:0, one launch (start us, length us, event | category | flops | bytes accessed | tf_op | source)
XLA Modules:
  0.0 199.7 jit_solution(3530504686131528474)
XLA Ops:
  0.6 62.6 %gather_and_forward.1 = (bf16[512,128]{1,0:T(8,128)(2,1)}, bf16[3,2048,256]{2,1,0:T(8,128)(2,1)}, bf16[256,2048]{1,0:T(8,128)(2,1)}, bf16[2048,1024]{1,0:T(8,128...) custom-call(bf16[1,128]{1,0:T(2,128)(2,1)} %bitcast.11, ...), custom_call_target="tpu_custom_call" | custom-call | tf_op jit(solution)/shard_map/gather_and_forward/pallas_call | solution.py:386
  63.3 127.5 %backward_and_sums.1 = (bf16[8,128,2048]{2,1,0:T(8,128)(2,1)}, bf16[8,128,2048]{2,1,0:T(8,128)(2,1)}, f32[128,1280]{1,0:T(8,128)}, f32[128,1024]{1,0:T(8,128)}, f32[128,768]{1,0:T(8,128)}, /*index=5*/f32[16,128]{1,0:T(8,128)}) custom-call(bf16[3,2048,256]{2,1,0:T(8,128)(2,1)} %get-tuple-element.40.wq_f, bf16[256,2048]{1,0:T(8,128)(2,1)} %get-tuple-element.41.wout_f, ...), custom_call_target="tpu_custom_call" | custom-call | tf_op jit(solution)/shard_map/backward_and_sums/pallas_call | solution.py:581
  190.8 8.7 %hand_over.1 = (bf16[1024,2048]{1,0:T(8,128)(2,1)}, bf16[1024,2048]{1,0:T(8,128)(2,1)}, f32[1,128]{1,0:T(1,128)}, f32[1,128]{1,0:T(1,128)}, f32[3,128,256]{2,1,0...) custom-call(bf16[8,128,2048]{2,1,0:T(8,128)(2,1)} %get-tuple-element, ...), custom_call_target="tpu_custom_call" | custom-call | tf_op jit(solution)/shard_map/hand_over/pallas_call | solution.py:637

commit v4 on v3

--- a/solution.py
+++ b/solution.py
@@ -31,7 +31,8 @@
     pl.semaphore_wait(bar, len(devices))
 
 class Gather:
-    def __init__(s, shard, full, axis, ss, rs):
+    def __init__(s, shard, full, axis, ss, rs, by_z=False):
+        s.by_z = by_z
         s.axis, s.ss, s.rs, s.full = axis, ss, rs, full
         s.c, s.y, s.zl, x, zh = place()
         c, y, zl = s.c, s.y, s.zl
@@ -62,7 +63,11 @@
     def serve(s):
         a = s.slot(0, 3); s.got(0, a); h = s.slot(0, 3, half=0); s.send(5, h, h, s.up)
         b = s.slot(0, 1); s.got(1, b); h = s.slot(0, 1, half=1); s.send(6, h, h, s.down)
-        z = s.slot(1, 0); s.got(2, z); s.send(3, z, z, s.up); s.send(4, z, z, s.down)
+        z = s.slot(1, 0); s.got(2, z)
+        if s.by_z:
+            s.send(3, a, a, s.z); s.send(4, b, b, s.z)
+        else:
+            s.send(3, z, z, s.up); s.send(4, z, z, s.down)
         s.relay(2); s.relay(1); s.relay(4)
     def serve2(s):
         s.got(5, s.slot(0, 2, half=0)); s.got(6, s.slot(0, 2, half=1))
@@ -251,7 +256,7 @@
     load(0, tok_h, tok); load(1, cot_h, cot); load(12, tab_h, tab)
     pack(vec, gain_s, lbias_s, bout_s, bdown_s, bup_s, bqkv_s)
     enter([peer(c, (y + 1) % 4, zl, x, zh), peer(c, (y + 3) % 4, zl, x, zh), peer(c, y, 1 - zl, x, zh), peer(1 - c, y, zl, x, zh)])
-    gv, gq, go, gu, gd = every = [Gather(a, b, ax, ss.at[i], rs.at[i]) for i, (a, b, ax) in enumerate(
+    gv, gq, go, gu, gd = every = [Gather(a, b, ax, ss.at[i], rs.at[i], i == 2) for i, (a, b, ax) in enumerate(
         [(vec, vecs, 0), (wq, wq_f, 2), (wout, wout_f, 1), (wup, wup_f, 0), (wdown, wdown_f, 1)])]
     local = [pltpu.make_async_copy(g.shard, g.slot(0, 0), ls.at[i]) for i, g in enumerate(every)]
     for cp in local: cp.start()
@@ -386,7 +391,7 @@
     return pl.pallas_call(forward_kernel,
         out_shape=[S((512, 128), bf16), S((3, 2048, 256), bf16), S((256, 2048), bf16), S((2048, 1024), bf16), S((1024, 2048), bf16),
                    S((8, 2048), f32), S((1024, 2048), bf16), S((1024, 256), bf16), S((1024, 1024), bf16), S((1024, 1024), bf16), S((1024, 768), bf16)],
-        in_specs=[V] * 6 + [A] * 7, out_specs=[A] * 11,
+        in_specs=[V] * 10 + [A] * 3, out_specs=[A] * 11,
         scratch_shapes=[vm((32, 128)), vm((3, 1024, 128), f32), vm((512, 128)), vm((3, 2048, 256)), vm((256, 2048)), vm((2048, 1024)), vm((1024, 2048)), vm((1024, 2048)), vm((1024, 2048)),
                         vm((8, 2048), f32), vm((8, 128), f32), vm((8, 1024), f32), vm((2, 1024, 128)), vm((2, 1024, 128)), vm((2, 1024, 128)), vm((2, 1024, 128)),
                         vm((1024, 256)), vm((2, 1024, 128), f32), vm((2, 1024, 128), f32), vm((1024, 768)), vm((1024, 1024)), vm((1024, 1024)),
@@ -593,17 +598,17 @@
 def hand_over_kernel(mixed, ingrad, o2_h, oup_h, oq_h, osv, mo, io, gg, gb, gq_h, gbq, go_h, gbo, gu_h, gbu, gd_h, gbd,
                      big, o2, oup, oq, gq, go, gd, li, lo):
     dp = lax.axis_index("dp")
-    def copy(a, b, sem):
-        cp = pltpu.make_async_copy(a, b, sem); cp.start()
+    def copy(a, b, sem, queue=0):
+        cp = pltpu.make_async_copy(a, b, sem); cp.start(priority=queue)
         return cp
     n = 8
-    ins = [copy((mixed, ingrad)[i // 4].at[pl.ds((i % 4) * 2, 2)], big.at[i], li.at[i]) for i in range(4)]
+    ins = [copy((mixed, ingrad)[i // 4].at[pl.ds((i % 4) * 2, 2)], big.at[i], li.at[i], i % 2) for i in range(4)]
     small = [copy(o2_h, o2, li.at[n]), copy(oup_h, oup, li.at[n + 1]), copy(oq_h, oq, li.at[n + 2])]
-    ins += [copy((mixed, ingrad)[i // 4].at[pl.ds((i % 4) * 2, 2)], big.at[i], li.at[i]) for i in range(4, 8)]
+    ins += [copy((mixed, ingrad)[i // 4].at[pl.ds((i % 4) * 2, 2)], big.at[i], li.at[i], i % 2) for i in range(4, 8)]
     outs = []
     def pass_on(i):
         ins[i].wait()
-        for h in range(2): outs.append(copy(big.at[i, h], (mo, io)[i // 4].at[pl.ds((i % 4) * 256 + h * 128, 128)], lo.at[2 * i + h]))
+        for h in range(2): outs.append(copy(big.at[i, h], (mo, io)[i // 4].at[pl.ds((i % 4) * 256 + h * 128, 128)], lo.at[2 * i + h], (i + 1) % 2))
     pass_on(0); pass_on(1)
     small[0].wait()
     for b in range(10):

time: 203 us -> 201 us (level)
  no operation moved by 1% of the time
where the time goes in v4:
time: 201 us; the launch traced here: 198 us
  Pallas kernels  197 us (98%)
    pallas_call x1, Pallas kernels, backward(): pl.pallas_call(backward_kernel, out_shape=[S((8, 128, 2048), bf16)] * 2 +...  128 us
    pallas_call x1, Pallas kernels, forward(): pl.pallas_call(forward_kernel, out_shape=[S((512, 128), bf16), S((3, 2048...  61.3 us
    pallas_call x1, Pallas kernels, hand_over(): pl.pallas_call(hand_over_kernel, out_shape=[S((1024, 2048), bf16)] * 2 +...  8.36 us

profile of v4, /device:TPU:0, one launch (start us, length us, event | category | flops | bytes accessed | tf_op | source)
XLA Modules:
  0.0 198.3 jit_solution(5582607042331899833)
XLA Ops:
  0.6 61.3 %gather_and_forward.1 = (bf16[512,128]{1,0:T(8,128)(2,1)}, bf16[3,2048,256]{2,1,0:T(8,128)(2,1)}, bf16[256,2048]{1,0:T(8,128)(2,1)}, bf16[2048,1024]{1,0:T(8,128...) custom-call(bf16[1,128]{1,0:T(2,128)(2,1)} %bitcast.11, ...), custom_call_target="tpu_custom_call" | custom-call | tf_op jit(solution)/shard_map/gather_and_forward/pallas_call | solution.py:391
  61.9 127.8 %backward_and_sums.1 = (bf16[8,128,2048]{2,1,0:T(8,128)(2,1)}, bf16[8,128,2048]{2,1,0:T(8,128)(2,1)}, f32[128,1280]{1,0:T(8,128)}, f32[128,1024]{1,0:T(8,128)}, f32[128,768]{1,0:T(8,128)}, /*index=5*/f32[16,128]{1,0:T(8,128)}) custom-call(bf16[3,2048,256]{2,1,0:T(8,128)(2,1)} %get-tuple-element.40.wq_f, bf16[256,2048]{1,0:T(8,128)(2,1)} %get-tuple-element.41.wout_f, ...), custom_call_target="tpu_custom_call" | custom-call | tf_op jit(solution)/shard_map/backward_and_sums/pallas_call | solution.py:586
  189.7 8.4 %hand_over.1 = (bf16[1024,2048]{1,0:T(8,128)(2,1)}, bf16[1024,2048]{1,0:T(8,128)(2,1)}, f32[1,128]{1,0:T(1,128)}, f32[1,128]{1,0:T(1,128)}, f32[3,128,256]{2,1,0...) custom-call(bf16[8,128,2048]{2,1,0:T(8,128)(2,1)} %get-tuple-element, ...), custom_call_target="tpu_custom_call" | custom-call | tf_op jit(solution)/shard_map/hand_over/pallas_call | solution.py:642

commit v5 on v4

--- a/solution.py
+++ b/solution.py
@@ -445,7 +445,7 @@
         for k, j in ((10, 4), (11, 2), (12, 3), (13, 5)): s.got(k, s.m.at[j])
         o = 1 - s.zl; b = s.b.at[4 + o]
         add_into(b, [b, s.m.at[2 + 2 * o], s.m.at[3 + 2 * o]], 128, 32); s.send(14, b, s.m.at[6], s.zn)
-    def serve4(s, put):
+    def serve4(s, put, step=32):
         s.got(14, s.m.at[6])
         z = s.zl
         terms = (s.b.at[4 + z], s.m.at[2 + 2 * z], s.m.at[3 + 2 * z], s.m.at[6])
@@ -453,7 +453,7 @@
             t = terms[0][r, :].astype(f32)
             for q in terms[1:]: t = t + q[r, :].astype(f32)
             put(r, t)
-        by_rows(128, 32, go)
+        by_rows(128, step, go)
 
 def backward_kernel(wq_f, wout_f, wup_f, wdown_f, rows_h, nrm_h, att_h, act_h, dact_h, gp_h, cot_h, tok_h,
                     mixed, ingrad, o2, oup, oq, osv,
@@ -550,7 +550,8 @@
             w = v.at[d % 2, d // 8, (d // 2) % 4]
             w[0:1, :] = sg[:, d * 128:(d + 1) * 128]; w[1:2, :] = sb[:, d * 128:(d + 1) * 128]
         sm.a()
-    def put2(r, t): o2[r, :] = t
+    def put2(r, t):
+        for b in range(10): o2[b * 128:(b + 1) * 128, :] = t[:, b * 128:(b + 1) * 128].T
     def putu(r, t): oup[r, :] = t
     def putq(r, t): oq[r, :] = t
     def xp(k): return (x + k) % 4
@@ -562,7 +563,7 @@
     steps = {"L0": first_loads, "L1": other_loads, "bA": far, "bB": near, "bC": near2, "bD": home, "gS": gn_start, "bias": bias_sums,
              "mS": mixed_start, "iS": ingrad_start, "va": norm_sums, "vb": sm.b, "vc": sm.c_, "vd": sm.d, "ve": sm.e, "vf": sm.f,
              "h0": partial(grad_hidden, 0, 1), "h1": partial(grad_hidden, 1, 2),
-             "s24": partial(s2.serve4, put2), "su4": partial(su.serve4, putu), "sq4": partial(sq.serve4, putq)}
+             "s24": partial(s2.serve4, put2, 128), "su4": partial(su.serve4, putu), "sq4": partial(sq.serve4, putq)}
     for i in range(4):
         steps["n%d" % i] = partial(grad_normed, i); steps["s2P%d" % i] = partial(s2.produce, cot, aa, i, i + 1)
     def up_grads(lo, hi):
@@ -584,7 +585,7 @@
     tsum = [vm((128, 2048)), vm((128, 2048)), vm((2, 2, 128, 2048)), vm((128, 2048)), vm((128, 2048))]
     A = pl.BlockSpec(memory_space=pl.ANY); V = pl.BlockSpec(memory_space=pltpu.VMEM)
     return pl.pallas_call(backward_kernel,
-        out_shape=[S((8, 128, 2048), bf16)] * 2 + [S((128, 1280), f32), S((128, 1024), f32), S((128, 768), f32), S((16, 128), f32)],
+        out_shape=[S((8, 128, 2048), bf16)] * 2 + [S((1280, 128), f32), S((128, 1024), f32), S((128, 768), f32), S((16, 128), f32)],
         in_specs=[A] * 12, out_specs=[A] * 2 + [V] * 4,
         scratch_shapes=[vm((1280, 2048)), vm((2, 512, 1792)), vm((1024, 2048)), vm((1024, 2048)), vm((1024, 1280)), vm((1024, 1792)),
                         vm((8, 2048), f32), vm((128, 2048)), vm((8, 128, 2048)), vm((8, 128, 2048)), vm((2, 128, 2048))]
@@ -596,7 +597,7 @@
         name="backward_and_sums")(wq_f, wout_f, wup_f, wdown_f, rows, nrm, att, act, dact, gp, cot, tok)
 
 def hand_over_kernel(mixed, ingrad, o2_h, oup_h, oq_h, osv, mo, io, gg, gb, gq_h, gbq, go_h, gbo, gu_h, gbu, gd_h, gbd,
-                     big, o2, oup, oq, gq, go, gd, li, lo):
+                     big, o2, oup, oq, li, lo):
     dp = lax.axis_index("dp")
     def copy(a, b, sem, queue=0):
         cp = pltpu.make_async_copy(a, b, sem); cp.start(priority=queue)
@@ -611,16 +612,11 @@
         for h in range(2): outs.append(copy(big.at[i, h], (mo, io)[i // 4].at[pl.ds((i % 4) * 256 + h * 128, 128)], lo.at[2 * i + h], (i + 1) % 2))
     pass_on(0); pass_on(1)
     small[0].wait()
-    for b in range(10):
-        t = o2[:, b * 128:(b + 1) * 128].T
-        if b < 2: go[b * 128:(b + 1) * 128, :] = t
-        else: gd[(b - 2) * 128:(b - 1) * 128, :] = t
-    outs += [copy(go, go_h, lo.at[16]), copy(gd, gd_h, lo.at[17])]
+    outs += [copy(o2.at[pl.ds(0, 256)], go_h, lo.at[16]), copy(o2.at[pl.ds(256, 1024)], gd_h, lo.at[17])]
     pass_on(2); pass_on(3)
     small[1].wait(); outs.append(copy(oup, gu_h, lo.at[18]))
     small[2].wait()
-    for j in range(3): gq[j] = oq[:, j * 256:(j + 1) * 256]
-    outs.append(copy(gq, gq_h, lo.at[19]))
+    for j in range(3): outs.append(copy(oq.at[:, pl.ds(j * 256, 256)], gq_h.at[j], lo.at[19 + j]))
     pass_on(4); pass_on(5)
     gg[...] = osv[0:1, :]; gb[...] = osv[1:2, :]; gbo[...] = osv[2:3, :]; gbd[...] = osv[2:3, :]
     l = lax.broadcasted_iota(jnp.int32, (128, 64), 0); k = lax.broadcasted_iota(jnp.int32, (128, 64), 1)
@@ -642,8 +638,8 @@
     return pl.pallas_call(hand_over_kernel,
         out_shape=[S((1024, 2048), bf16)] * 2 + [S(sh, f32) for sh, _ in outs],
         in_specs=[A] * 5 + [full((16, 128))], out_specs=[A] * 2 + [A if m else full(sh) for sh, m in outs],
-        scratch_shapes=[pltpu.VMEM((8, 2, 128, 2048), bf16), vm((128, 1280)), vm((128, 1024)), vm((128, 768)), vm((3, 128, 256)), vm((256, 128)), vm((1024, 128)),
-                        pltpu.SemaphoreType.DMA((12,)), pltpu.SemaphoreType.DMA((20,))],
+        scratch_shapes=[pltpu.VMEM((8, 2, 128, 2048), bf16), vm((1280, 128)), vm((128, 1024)), vm((128, 768)),
+                        pltpu.SemaphoreType.DMA((12,)), pltpu.SemaphoreType.DMA((22,))],
         compiler_params=pltpu.CompilerParams(vmem_limit_bytes=62 << 20),
         name="hand_over")(mixed, ingrad, o2, oup, oq, osv)
 

time: 201 us -> 201 us (level)
  no operation moved by 1% of the time
where the time goes in v5:
time: 201 us; the launch traced here: 198 us
  Pallas kernels  197 us (98%)
    pallas_call x1, Pallas kernels, backward(): pl.pallas_call(backward_kernel, out_shape=[S((8, 128, 2048), bf16)] * 2 +...  128 us
    pallas_call x1, Pallas kernels, forward(): pl.pallas_call(forward_kernel, out_shape=[S((512, 128), bf16), S((3, 2048...  61.3 us
    pallas_call x1, Pallas kernels, hand_over(): pl.pallas_call(hand_over_kernel, out_shape=[S((1024, 2048), bf16)] * 2 +...  8.38 us

profile of v5, /device:TPU:0, one launch (start us, length us, event | category | flops | bytes accessed | tf_op | source)
XLA Modules:
  0.0 198.3 jit_solution(8388739604774508117)
XLA Ops:
  0.6 61.3 %gather_and_forward.1 = (bf16[512,128]{1,0:T(8,128)(2,1)}, bf16[3,2048,256]{2,1,0:T(8,128)(2,1)}, bf16[256,2048]{1,0:T(8,128)(2,1)}, bf16[2048,1024]{1,0:T(8,128...) custom-call(bf16[1,128]{1,0:T(2,128)(2,1)} %bitcast.11, ...), custom_call_target="tpu_custom_call" | custom-call | tf_op jit(solution)/shard_map/gather_and_forward/pallas_call | solution.py:391
  61.9 127.8 %backward_and_sums.1 = (bf16[8,128,2048]{2,1,0:T(8,128)(2,1)}, bf16[8,128,2048]{2,1,0:T(8,128)(2,1)}, f32[1280,128]{1,0:T(8,128)}, f32[128,1024]{1,0:T(8,128)}, f32[128,768]{1,0:T(8,128)}, /*index=5*/f32[16,128]{1,0:T(8,128)}) custom-call(bf16[3,2048,256]{2,1,0:T(8,128)(2,1)} %get-tuple-element.40.wq_f, bf16[256,2048]{1,0:T(8,128)(2,1)} %get-tuple-element.41.wout_f, ...), custom_call_target="tpu_custom_call" | custom-call | tf_op jit(solution)/shard_map/backward_and_sums/pallas_call | solution.py:587
  189.7 8.4 %hand_over.1 = (bf16[1024,2048]{1,0:T(8,128)(2,1)}, bf16[1024,2048]{1,0:T(8,128)(2,1)}, f32[1,128]{1,0:T(1,128)}, f32[1,128]{1,0:T(1,128)}, f32[3,128,256]{2,1,0...) custom-call(bf16[8,128,2048]{2,1,0:T(8,128)(2,1)} %get-tuple-element, ...), custom_call_target="tpu_custom_call" | custom-call | tf_op jit(solution)/shard_map/hand_over/pallas_call | solution.py:638
